TPU v7x, 32 devices: a whole 2x2x4 slice. The times are simulated.
32 devices in a mesh: grp: 2 (over y), stn: 16 (over z, x, core).
Axes of the slice: x: 2, y: 2, z: 4, core: 2. Of those that a mesh axis runs over, the one named last changes fastest.
Arguments:
- pair_uvw_coordinates: float32 [3, 4096], P(None, ('grp', 'stn')), parts along dimension 1, may hold values from -120 to 120
- directions: float32 [2, 128], replicated, may hold values from -0.4 to 0.4
- brightness: float32 [8, 32, 128], replicated, may hold values from -0.4 to 0.4
- observed: float32 [32, 8, 4096], P(None, None, ('grp', 'stn')), parts along dimension 2, may hold values from -6 to 6
- coefficients: float32 [64, 24, 128], P(('grp', 'stn')), parts along dimension 0, may hold values from -1.5 to 2.5
- station_pair: int32 [2, 4096], P(None, ('grp', 'stn')), parts along dimension 1, may hold values from 0 to 31, as said below
Outputs:
- gradient: float32 [64, 24, 128], P(('grp', 'stn')), parts along dimension 0
- residual: float32 [32, 8, 4096], P(None, None, ('grp', 'stn')), parts along dimension 2
There are 2 independent parts, one for each index of `grp`. A program takes and returns all parts, laid end to end along the dimension named above; an argument that names none is the same for every part. Nothing has to cross between parts.
Inputs may be any that keep to these rules, and one draw needn't show every extreme that they name: `station_pair`: the two stations of a baseline differ.
All inputs are finite; a program needn't handle non-finite values.
Results may differ from a plain program's by a relative error of at most 0.0003.
Values sent between devices are 32-bit elements; how exact they have to be, the bound alone decides.
A program may use at most 128 MiB of HBM per device.

v0:
```python
import math

import jax
import jax.numpy as jnp
from jax import lax
from jax.sharding import PartitionSpec as P


def powers_of(frequency_number, degree_count):
    channel_pos = jnp.arange(frequency_number, dtype=jnp.float32)
    centre = (2.0 * channel_pos - (frequency_number - 1)) / max(frequency_number - 1, 1)
    levels = [jnp.ones_like(centre)]
    for degree in range(1, degree_count):
        levels.append(levels[-1] * centre)
    return (jnp.stack(levels), 1.0 + 0.25 * centre)


def evaluate(coeff_table, powers):
    degree_count = powers.shape[0]
    shaped = coeff_table.reshape(coeff_table.shape[0], degree_count, 8, coeff_table.shape[2])
    result = shaped[:, 0][:, None] * powers[0][None, :, None, None]
    for degree in range(1, degree_count):
        result = result + shaped[:, degree][:, None] * powers[degree][None, :, None, None]
    return result


def contract(grads, powers):
    pieces = [
        jnp.sum(grads * powers[degree][None, :, None, None], axis=1)
        for degree in range(powers.shape[0])
    ]
    stacked = jnp.stack(pieces, axis=1)
    return stacked.reshape(stacked.shape[0], stacked.shape[1] * 8, stacked.shape[3])


def mat_product(left_re, left_im, right_re, right_im):
    first_re = left_re[:, 0:1] * right_re[0:1] - left_im[:, 0:1] * right_im[0:1]
    second_re = left_re[:, 1:2] * right_re[1:2] - left_im[:, 1:2] * right_im[1:2]
    first_im = left_re[:, 0:1] * right_im[0:1] + left_im[:, 0:1] * right_re[0:1]
    second_im = left_re[:, 1:2] * right_im[1:2] + left_im[:, 1:2] * right_re[1:2]
    return (first_re + second_re, first_im + second_im)


def adjoint(matrix_re, matrix_im):
    return (jnp.swapaxes(matrix_re, 0, 1), -jnp.swapaxes(matrix_im, 0, 1))


def to_matrix(jones_rows):
    shaped = jones_rows.reshape(
        jones_rows.shape[0], jones_rows.shape[1], 2, 2, 2, jones_rows.shape[3]
    )
    real_part = jnp.transpose(shaped[:, :, :, :, 0], (2, 3, 0, 1, 4))
    imag_part = jnp.transpose(shaped[:, :, :, :, 1], (2, 3, 0, 1, 4))
    return (real_part, imag_part)


def from_matrix(real_part, imag_part):
    stacked = jnp.stack((real_part, imag_part), axis=2)
    reordered = jnp.transpose(stacked, (3, 4, 0, 1, 2, 5))
    return reordered.reshape(reordered.shape[0], reordered.shape[1], 8, reordered.shape[5])


def baseline_terms(jones_near, jones_far, coords, directions, brightness, observed, freq_ratio):
    frequency_number = brightness.shape[1]
    dir_count = brightness.shape[2]
    entries_in_tile = coords.shape[1]
    depth_term = jnp.sqrt(1.0 - directions[0] * directions[0] - directions[1] * directions[1]) - 1.0
    inner_sum = (
        coords[0][:, None] * directions[0][None, :]
        + coords[1][:, None] * directions[1][None, :]
        + coords[2][:, None] * depth_term[None, :]
    )
    phase_angle = 2.0 * math.pi * freq_ratio[None, :, None] * inner_sum[:, None, :]
    cosine = jnp.cos(phase_angle)
    sine_part = jnp.sin(phase_angle)
    bright = brightness.reshape(2, 2, 2, frequency_number, dir_count)
    bright_re = bright[:, :, 0][:, :, None]
    bright_im = bright[:, :, 1][:, :, None]
    coh_re = bright_re * cosine + bright_im * sine_part
    coh_im = bright_im * cosine - bright_re * sine_part
    near_re, near_im = to_matrix(jones_near)
    far_re, far_im = to_matrix(jones_far)
    left_re, left_im = mat_product(near_re, near_im, coh_re, coh_im)
    fadj_re, fadj_im = adjoint(far_re, far_im)
    model_re, model_im = mat_product(left_re, left_im, fadj_re, fadj_im)
    cadj_re, cadj_im = adjoint(coh_re, coh_im)
    right_re, right_im = mat_product(far_re, far_im, cadj_re, cadj_im)
    seen_block = observed.reshape(frequency_number, 2, 2, 2, entries_in_tile)
    diff_re = jnp.transpose(seen_block[:, :, :, 0], (1, 2, 3, 0)) - jnp.sum(model_re, axis=-1)
    diff_im = jnp.transpose(seen_block[:, :, :, 1], (1, 2, 3, 0)) - jnp.sum(model_im, axis=-1)
    radj_re, radj_im = adjoint(diff_re, diff_im)
    gnear_re, gnear_im = mat_product(diff_re[..., None], diff_im[..., None], right_re, right_im)
    gfar_re, gfar_im = mat_product(radj_re[..., None], radj_im[..., None], left_re, left_im)
    stacked = jnp.stack((diff_re, diff_im), axis=2)
    resid_block = jnp.transpose(stacked, (4, 0, 1, 2, 3)).reshape(
        frequency_number, 8, entries_in_tile
    )
    return (resid_block, from_matrix(-gnear_re, -gnear_im), from_matrix(-gfar_re, -gfar_im))


def segment_rows(values, stations, row_count):
    inside = (stations >= 0) & (stations < row_count)
    target = jnp.where(inside, stations, row_count)
    return jax.ops.segment_sum(values, target, num_segments=row_count + 1)[:row_count]


def shards(pair_uvw_coordinates, directions, brightness, observed, coefficients, station_pair):
    frequency_number = brightness.shape[1]
    dir_count = brightness.shape[2]
    degree_count = coefficients.shape[1] // 8
    stations_dev = coefficients.shape[0]
    pairs_held_here = pair_uvw_coordinates.shape[1]
    powers, freq_ratio = powers_of(frequency_number, degree_count)
    jones_all = evaluate(lax.all_gather(coefficients, "stn", axis=0, tiled=True), powers)
    entries_in_tile = math.gcd(pairs_held_here, 32)
    rotation_number = pairs_held_here // entries_in_tile
    coords_blocks = jnp.transpose(
        pair_uvw_coordinates.reshape(3, rotation_number, entries_in_tile), (1, 0, 2)
    )
    seen_blocks = jnp.transpose(
        observed.reshape(frequency_number, 8, rotation_number, entries_in_tile), (2, 0, 1, 3)
    )
    near_blocks = station_pair[0].reshape(rotation_number, entries_in_tile)
    far_blocks = station_pair[1].reshape(rotation_number, entries_in_tile)

    def visit_block(pieces):
        coords, seen_block, pick_near, pick_far = pieces
        resid_block, slope_first_antenna, slope_second_antenna = baseline_terms(
            jnp.take(jones_all, pick_near, axis=0),
            jnp.take(jones_all, pick_far, axis=0),
            coords,
            directions,
            brightness,
            seen_block,
            freq_ratio,
        )
        slope_first_antenna = contract(slope_first_antenna, powers)
        slope_second_antenna = contract(slope_second_antenna, powers)
        return (
            resid_block,
            slope_first_antenna.reshape(entries_in_tile, -1),
            slope_second_antenna.reshape(entries_in_tile, -1),
        )

    residual_blocks, slope_first_antenna, slope_second_antenna = lax.map(
        visit_block, (coords_blocks, seen_blocks, near_blocks, far_blocks)
    )
    slope_first_antenna = slope_first_antenna.reshape(pairs_held_here, slope_first_antenna.shape[2])
    slope_second_antenna = slope_second_antenna.reshape(
        pairs_held_here, slope_second_antenna.shape[2]
    )
    summed = lax.psum_scatter(
        segment_rows(slope_first_antenna, station_pair[0], lax.axis_size("stn") * stations_dev)
        + segment_rows(slope_second_antenna, station_pair[1], lax.axis_size("stn") * stations_dev),
        "stn",
        scatter_dimension=0,
        tiled=True,
    )
    gradient = summed.reshape(stations_dev, degree_count * 8, dir_count)
    residual = jnp.transpose(residual_blocks, (1, 2, 0, 3)).reshape(
        frequency_number, 8, pairs_held_here
    )
    return (gradient, residual)


def solution(mesh):
    placed = (
        P(None, ("grp", "stn")),
        P(),
        P(),
        P(None, None, ("grp", "stn")),
        P(("grp", "stn"), None, None),
        P(None, ("grp", "stn")),
    )
    return jax.shard_map(
        shards,
        mesh=mesh,
        in_specs=placed,
        out_specs=(P(("grp", "stn"), None, None), P(None, None, ("grp", "stn"))),
        check_vma=False,
    )
```

profile of v0, /device:TPU:0, one launch (start us, length us, event | category | flops | bytes accessed | tf_op | source)
XLA Modules:
  0.0 408.7 jit_solution(4881080389891526292)
XLA Ops:
  9.4 2.0 reshape.374
  14.8 24.4 %all_gather.3 = f32[32,24,128]{2,1,0:T(8,128)S(1)} all-gather(f32[2,24,128]{2,1,0:T(8,128)} %param.14), channel_id=1, replica_groups=mesh['grp'=2,'stn'=16] {'stn'}, dimensions={0}, use_global_device_ids=true | all-gather | bytes 417792 | tf_op jit(solution)/shard_map/all_gather | solution.py:114
  39.2 265.2 %while.18 = (s32[]{:T(128)}, f32[4,32,8,32]{3,1,2,0:T(8,128)}, f32[4,32,3072]{2,1,0:T(8,128)}, f32[4,32,3072]{2,1,0:T(8,128)}, f32[4,32,8,32]{3,0,2,1:T(4,128)},...) while((s32[]{:T(128)}, f32[4,32,8,32]{3,1,2,0:T(8,128)}, ...), condition=%wide.region_9.11_spmd.clone.clone, body=%wide.region_0.10_spmd.clone.clone.sunk | while | flops 66432132 | bytes 291259232 | solution.py:145
  40.7 1.9 multiply_cosine_fusion.2
  43.5 2.9 multiply_add_fusion.9
  47.7 1.5 slice_bitcast_fusion.81
  49.3 2.8 multiply_add_fusion.10
  52.7 5.0 %gather_fusion = f32[32,32,8,128]{3,2,1,0:T(8,128)} fusion(f32[32,32,8,128]{3,2,1,0:T(8,128)} %multiply_add_fusion.10, s32[1024]{0:T(1024)S(1)} %pad_clamp_fusion.4), kind=kCustom, calls=%fused_computation.clone.clone.1 | custom fusion | bytes 8388736 | tf_op jit(solution)/shard_map/while/body/eval_jaxpr/jit(_take)/gather | solution.py:129
  57.7 2.7 broadcast_select_fusion.4
  66.6 1.5 slice_bitcast_fusion.86
  68.8 5.0 %gather_fusion.1 = f32[32,32,8,128]{3,2,1,0:T(8,128)} fusion(f32[32,32,8,128]{3,2,1,0:T(8,128)} %multiply_add_fusion.10, s32[1024]{0:T(1024)S(1)} %pad_clamp_fusion.5), kind=kCustom, calls=%fused_computation.1.clone.clone.1 | custom fusion | bytes 8388736 | tf_op jit(solution)/shard_map/while/body/eval_jaxpr/jit(_take)/gather | solution.py:130
  73.8 2.7 broadcast_select_fusion.5
  77.2 2.5 slice_bitcast_fusion.87
  82.2 2.0 add_reduce_fusion.3
  86.4 1.8 slice_bitcast_fusion.90
  90.2 1.4 copy-done.1
  91.8 1.4 copy-done.4
  98.0 5.8 %fusion.94 = (f32[32,2,2,2,128]{4,0,3,2,1:T(8,128)S(1)}, f32[32,2,2,2,128]{4,0,3,2,1:T(8,128)S(1)}, f32[32,2,2,2,128]{4,0,3,2,1:T(8,128)S(1)}, f32[32,2,2,2,128]...) fusion(f32[2,2,1,32,32,128]{5,4,3,2,1,0:T(8,128)S(1)} %get-tuple-element.764, ...), kind=kLoop, calls=%fused_computation.15.clone.1 | loop fusion | flops 12386304 | bytes 9175296 | tf_op jit(solution)/shard_map/while/body/eval_jaxpr/reduce_sum | solution.py:29
  107.0 1.9 multiply_cosine_fusion.2
  109.8 2.9 multiply_add_fusion.9
  114.0 1.5 slice_bitcast_fusion.81
  115.6 2.8 multiply_add_fusion.10
  119.0 5.0 %gather_fusion = f32[32,32,8,128]{3,2,1,0:T(8,128)} fusion(f32[32,32,8,128]{3,2,1,0:T(8,128)} %multiply_add_fusion.10, s32[1024]{0:T(1024)S(1)} %pad_clamp_fusion.4), kind=kCustom, calls=%fused_computation.clone.clone.1 | custom fusion | bytes 8388736 | tf_op jit(solution)/shard_map/while/body/eval_jaxpr/jit(_take)/gather | solution.py:129
  124.0 2.7 broadcast_select_fusion.4
  132.9 1.5 slice_bitcast_fusion.86
  135.1 5.0 %gather_fusion.1 = f32[32,32,8,128]{3,2,1,0:T(8,128)} fusion(f32[32,32,8,128]{3,2,1,0:T(8,128)} %multiply_add_fusion.10, s32[1024]{0:T(1024)S(1)} %pad_clamp_fusion.5), kind=kCustom, calls=%fused_computation.1.clone.clone.1 | custom fusion | bytes 8388736 | tf_op jit(solution)/shard_map/while/body/eval_jaxpr/jit(_take)/gather | solution.py:130
  140.1 2.7 broadcast_select_fusion.5
  143.5 2.5 slice_bitcast_fusion.87
  148.5 2.0 add_reduce_fusion.3
  152.7 1.8 slice_bitcast_fusion.90
  156.5 1.4 copy-done.1
  164.3 5.8 %fusion.94 = (f32[32,2,2,2,128]{4,0,3,2,1:T(8,128)S(1)}, f32[32,2,2,2,128]{4,0,3,2,1:T(8,128)S(1)}, f32[32,2,2,2,128]{4,0,3,2,1:T(8,128)S(1)}, f32[32,2,2,2,128]...) fusion(f32[2,2,1,32,32,128]{5,4,3,2,1,0:T(8,128)S(1)} %get-tuple-element.764, ...), kind=kLoop, calls=%fused_computation.15.clone.1 | loop fusion | flops 12386304 | bytes 9175296 | tf_op jit(solution)/shard_map/while/body/eval_jaxpr/reduce_sum | solution.py:29
  173.3 1.9 multiply_cosine_fusion.2
  176.1 2.9 multiply_add_fusion.9
  180.3 1.5 slice_bitcast_fusion.81
  181.9 2.8 multiply_add_fusion.10
  185.3 5.0 %gather_fusion = f32[32,32,8,128]{3,2,1,0:T(8,128)} fusion(f32[32,32,8,128]{3,2,1,0:T(8,128)} %multiply_add_fusion.10, s32[1024]{0:T(1024)S(1)} %pad_clamp_fusion.4), kind=kCustom, calls=%fused_computation.clone.clone.1 | custom fusion | bytes 8388736 | tf_op jit(solution)/shard_map/while/body/eval_jaxpr/jit(_take)/gather | solution.py:129
  190.3 2.7 broadcast_select_fusion.4
  199.2 1.5 slice_bitcast_fusion.86
  201.4 5.0 %gather_fusion.1 = f32[32,32,8,128]{3,2,1,0:T(8,128)} fusion(f32[32,32,8,128]{3,2,1,0:T(8,128)} %multiply_add_fusion.10, s32[1024]{0:T(1024)S(1)} %pad_clamp_fusion.5), kind=kCustom, calls=%fused_computation.1.clone.clone.1 | custom fusion | bytes 8388736 | tf_op jit(solution)/shard_map/while/body/eval_jaxpr/jit(_take)/gather | solution.py:130
  206.4 2.7 broadcast_select_fusion.5
  209.8 2.5 slice_bitcast_fusion.87
  214.8 2.0 add_reduce_fusion.3
  219.0 1.8 slice_bitcast_fusion.90
  222.8 1.4 copy-done.1
  224.4 1.4 copy-done.4
  230.6 5.8 %fusion.94 = (f32[32,2,2,2,128]{4,0,3,2,1:T(8,128)S(1)}, f32[32,2,2,2,128]{4,0,3,2,1:T(8,128)S(1)}, f32[32,2,2,2,128]{4,0,3,2,1:T(8,128)S(1)}, f32[32,2,2,2,128]...) fusion(f32[2,2,1,32,32,128]{5,4,3,2,1,0:T(8,128)S(1)} %get-tuple-element.764, ...), kind=kLoop, calls=%fused_computation.15.clone.1 | loop fusion | flops 12386304 | bytes 9175296 | tf_op jit(solution)/shard_map/while/body/eval_jaxpr/reduce_sum | solution.py:29
  239.6 1.9 multiply_cosine_fusion.2
  242.4 2.9 multiply_add_fusion.9
  246.6 1.5 slice_bitcast_fusion.81
  248.2 2.8 multiply_add_fusion.10
  251.6 5.0 %gather_fusion = f32[32,32,8,128]{3,2,1,0:T(8,128)} fusion(f32[32,32,8,128]{3,2,1,0:T(8,128)} %multiply_add_fusion.10, s32[1024]{0:T(1024)S(1)} %pad_clamp_fusion.4), kind=kCustom, calls=%fused_computation.clone.clone.1 | custom fusion | bytes 8388736 | tf_op jit(solution)/shard_map/while/body/eval_jaxpr/jit(_take)/gather | solution.py:129
  256.6 2.7 broadcast_select_fusion.4
  265.5 1.5 slice_bitcast_fusion.86
  267.7 5.0 %gather_fusion.1 = f32[32,32,8,128]{3,2,1,0:T(8,128)} fusion(f32[32,32,8,128]{3,2,1,0:T(8,128)} %multiply_add_fusion.10, s32[1024]{0:T(1024)S(1)} %pad_clamp_fusion.5), kind=kCustom, calls=%fused_computation.1.clone.clone.1 | custom fusion | bytes 8388736 | tf_op jit(solution)/shard_map/while/body/eval_jaxpr/jit(_take)/gather | solution.py:130
  272.7 2.7 broadcast_select_fusion.5
  276.1 2.5 slice_bitcast_fusion.87
  281.1 2.0 add_reduce_fusion.3
  285.3 1.8 slice_bitcast_fusion.90
  290.7 1.4 copy-done.4
  296.9 5.8 %fusion.94 = (f32[32,2,2,2,128]{4,0,3,2,1:T(8,128)S(1)}, f32[32,2,2,2,128]{4,0,3,2,1:T(8,128)S(1)}, f32[32,2,2,2,128]{4,0,3,2,1:T(8,128)S(1)}, f32[32,2,2,2,128]...) fusion(f32[2,2,1,32,32,128]{5,4,3,2,1,0:T(8,128)S(1)} %get-tuple-element.764, ...), kind=kLoop, calls=%fused_computation.15.clone.1 | loop fusion | flops 12386304 | bytes 9175296 | tf_op jit(solution)/shard_map/while/body/eval_jaxpr/reduce_sum | solution.py:29
  304.4 3.7 scatter_custom_fusion.1
  308.1 3.6 scatter_custom_fusion
  315.0 85.3 %all-reduce.3.cloned.1.call-done = f32[32,3072]{1,0:T(8,128)} async-done(((f32[32,3072]{1,0:T(8,128)}), f32[32,3072]{1,0:T(8,128)}) %all-reduce.3.cloned.1.call-update) | async-done | bytes 393232
  (345 shorter events, 112.6 us)
Async XLA Ops:
  7.2 393.2 %all-reduce.3.cloned.1.call-start = ((), (), s32[]{:S(2)}) async-start(), calls=%async_computation | async-start | bytes 786432
  39.2 10.1 %copy-start.11 = (f32[32,8,128]{2,1,0:T(8,128)}, f32[32,8,128]{2,1,0:T(8,128)S(1)}, u32[]{:S(2)}) copy-start(f32[32,8,128]{2,1,0:T(8,128)S(1)} %get-tuple-element.856) | copy-start | bytes 393220 | tf_op jit(solution)/shard_map/while
  62.0 1.2 copy-start.5
  62.0 1.5 copy-start.6
  62.0 1.8 copy-start.7
  65.0 1.7 copy-start
  80.3 1.2 copy-start.8
  80.4 1.5 copy-start.9
  80.4 1.8 copy-start.10
  88.4 1.6 copy-start.2
  90.0 1.6 copy-start.1
  91.6 1.6 copy-start.4
  93.2 1.6 copy-start.3
  104.2 1.3 copy-start.12
  105.5 10.1 %copy-start.11 = (f32[32,8,128]{2,1,0:T(8,128)}, f32[32,8,128]{2,1,0:T(8,128)S(1)}, u32[]{:S(2)}) copy-start(f32[32,8,128]{2,1,0:T(8,128)S(1)} %get-tuple-element.856) | copy-start | bytes 393220 | tf_op jit(solution)/shard_map/while
  128.3 1.2 copy-start.5
  128.3 1.5 copy-start.6
  128.3 1.8 copy-start.7
  131.3 1.7 copy-start
  146.6 1.2 copy-start.8
  146.6 1.5 copy-start.9
  146.7 1.8 copy-start.10
  154.7 1.6 copy-start.2
  156.3 1.6 copy-start.1
  157.9 1.6 copy-start.4
  159.5 1.6 copy-start.3
  170.5 1.3 copy-start.12
  171.8 10.1 %copy-start.11 = (f32[32,8,128]{2,1,0:T(8,128)}, f32[32,8,128]{2,1,0:T(8,128)S(1)}, u32[]{:S(2)}) copy-start(f32[32,8,128]{2,1,0:T(8,128)S(1)} %get-tuple-element.856) | copy-start | bytes 393220 | tf_op jit(solution)/shard_map/while
  194.6 1.2 copy-start.5
  194.6 1.5 copy-start.6
  194.6 1.8 copy-start.7
  197.5 1.7 copy-start
  212.9 1.2 copy-start.8
  212.9 1.5 copy-start.9
  212.9 1.8 copy-start.10
  221.0 1.6 copy-start.2
  222.6 1.6 copy-start.1
  224.2 1.6 copy-start.4
  225.8 1.6 copy-start.3
  236.8 1.3 copy-start.12
  238.1 10.1 %copy-start.11 = (f32[32,8,128]{2,1,0:T(8,128)}, f32[32,8,128]{2,1,0:T(8,128)S(1)}, u32[]{:S(2)}) copy-start(f32[32,8,128]{2,1,0:T(8,128)S(1)} %get-tuple-element.856) | copy-start | bytes 393220 | tf_op jit(solution)/shard_map/while
  260.9 1.2 copy-start.5
  260.9 1.5 copy-start.6
  260.9 1.8 copy-start.7
  263.8 1.7 copy-start
  279.2 1.2 copy-start.8
  279.2 1.5 copy-start.9
  279.2 1.8 copy-start.10
  287.3 1.6 copy-start.2
  288.9 1.6 copy-start.1
  290.5 1.6 copy-start.4
  292.1 1.6 copy-start.3
  303.1 1.3 copy-start.12
  304.4 8.1 %copy-start.13 = (f32[4,32,8,32]{3,1,2,0:T(8,128)S(1)}, f32[4,32,8,32]{3,1,2,0:T(8,128)}, u32[]{:S(2)}) copy-start(f32[4,32,8,32]{3,1,2,0:T(8,128)} %get-tuple-element.197) | copy-start | bytes 393220
  304.4 9.4 %copy-start.14 = (u32[32]{0:T(128)S(1)}, u32[32]{0:T(128)}, u32[]{:S(2)}) copy-start(u32[32]{0:T(128)} %constant.79) | copy-start | bytes 388
Sparse Core Ops, SparseCore 0:
  312.6 87.6 all-reduce.2
where the time goes:
time: 411 us; the launch traced here: 409 us
  local copies, waits for them, and re-layouts  158 us (38%)
  other arithmetic  124 us (30%)
  waiting for transfers between devices  85.3 us (21%)
  blocking collectives  24.4 us (6%)
  between operations  14.8 us (4%)
    unnamed x2, waiting for transfers between devices  85.3 us
    mul x80, local copies, waits for them, and re-layouts, mat_product(): first_re = left_re[:, 0:1] * right_re[0:1] - left_im[:, 0:1] * right_im[0:1]  38.5 us
    while x112, local copies, waits for them, and re-layouts  32.1 us
    all_gather x1, blocking collectives, shards(): lax.all_gather(coefficients, 'stn', axis=0, tiled=True)  24.4 us
    reduce_sum x4, other arithmetic, contract(): jnp.sum(grads * powers[degree][None, :, None, None], axis=1)  23.4 us
    gather x4, local copies, waits for them, and re-layouts, visit_block(): jnp.take(jones_all, pick_near, axis=0)  20 us
    gather x4, local copies, waits for them, and re-layouts, visit_block(): jnp.take(jones_all, pick_far, axis=0)  20 us
    transpose x8, local copies, waits for them, and re-layouts, to_matrix(): real_part = jnp.transpose(shaped[:, :, :, :, 0], (2, 3, 0, 1, 4))  12.7 us
  transfers between devices with their start and end apart: 1, of which 1 were waited for; matrix products, arithmetic and copies ran while one was open for 0% of the time, Pallas kernels for 0%

commit v1 on v0

--- a/solution.py
+++ b/solution.py
@@ -1,9 +1,17 @@
+import functools
 import math
 
 import jax
 import jax.numpy as jnp
 from jax import lax
+from jax.experimental import pallas as pl
+from jax.experimental.pallas import tpu as pltpu
 from jax.sharding import PartitionSpec as P
+
+MESH = pl.DeviceIdType.MESH
+LANES = 128
+ROWS = 8
+VMEM_BUDGET = 44 * 1024 * 1024
 
 
 def powers_of(frequency_number, degree_count):
@@ -104,7 +112,7 @@
     return jax.ops.segment_sum(values, target, num_segments=row_count + 1)[:row_count]
 
 
-def shards(pair_uvw_coordinates, directions, brightness, observed, coefficients, station_pair):
+def general_shards(pair_uvw_coordinates, directions, brightness, observed, coefficients, station_pair):
     frequency_number = brightness.shape[1]
     dir_count = brightness.shape[2]
     degree_count = coefficients.shape[1] // 8
@@ -163,6 +171,336 @@
     return (gradient, residual)
 
 
+def greet(n):
+    me = lax.axis_index("stn")
+    barrier = pltpu.get_barrier_semaphore()
+    for d in range(1, n):
+        pl.semaphore_signal(
+            barrier, inc=1, device_id={"stn": lax.rem(me + d, n)}, device_id_type=MESH
+        )
+    pl.semaphore_wait(barrier, n - 1)
+    return me
+
+
+def gather_kernel(n, own_ref, all_ref, send_sem, recv_sem):
+    me = greet(n)
+    copies = []
+    for d in range(1, n):
+        copy = pltpu.make_async_remote_copy(
+            src_ref=own_ref,
+            dst_ref=all_ref.at[me],
+            send_sem=send_sem.at[d],
+            recv_sem=recv_sem.at[d],
+            device_id={"stn": lax.rem(me + d, n)},
+            device_id_type=MESH,
+        )
+        copy.start()
+        copies.append(copy)
+    all_ref[me] = own_ref[...]
+    for copy in copies:
+        copy.wait()
+
+
+def scatter_sum_kernel(n, part_ref, sum_ref, held, send_sem, recv_sem):
+    me = greet(n)
+    copies = []
+    for d in range(1, n):
+        peer = lax.rem(me + d, n)
+        copy = pltpu.make_async_remote_copy(
+            src_ref=part_ref.at[peer],
+            dst_ref=held.at[d],
+            send_sem=send_sem.at[d],
+            recv_sem=recv_sem.at[d],
+            device_id={"stn": peer},
+            device_id_type=MESH,
+        )
+        copy.start()
+        copies.append(copy)
+    total = part_ref[me]
+    for d, copy in enumerate(copies, 1):
+        copy.wait_recv()
+        total = total + held[d]
+    sum_ref[...] = total
+    for copy in copies:
+        copy.wait_send()
+
+
+def turn_sin_cos(turns):
+    x = math.pi * (turns - jnp.round(turns))
+    y = x * x
+    s = jnp.full_like(y, -1.0 / math.factorial(11))
+    for k in (9, 7, 5, 3, 1):
+        s = s * y + (1.0 if k % 4 == 1 else -1.0) / math.factorial(k)
+    s = s * x
+    c = jnp.full_like(y, 1.0 / math.factorial(12))
+    for k in (10, 8, 6, 4, 2, 0):
+        c = c * y + (1.0 if k % 4 == 0 else -1.0) / math.factorial(k)
+    return 2.0 * (s * c), 1.0 - 2.0 * (s * s)
+
+
+def times(left, right):
+    out = []
+    for i in range(2):
+        for j in range(2):
+            (ar, ai), (br, bi) = left[2 * i], right[j]
+            (cr, ci), (dr, di) = left[2 * i + 1], right[2 + j]
+            out.append(
+                (
+                    (ar * br - ai * bi) + (cr * dr - ci * di),
+                    (ar * bi + ai * br) + (cr * di + ci * dr),
+                )
+            )
+    return out
+
+
+def times_adj(left, right):
+    out = []
+    for i in range(2):
+        for j in range(2):
+            (ar, ai), (br, bi) = left[2 * i], right[2 * j]
+            (cr, ci), (dr, di) = left[2 * i + 1], right[2 * j + 1]
+            out.append(
+                (
+                    (ar * br + ai * bi) + (cr * dr + ci * di),
+                    (ai * br - ar * bi) + (ci * dr - cr * di),
+                )
+            )
+    return out
+
+
+def adj_times(left, right):
+    out = []
+    for i in range(2):
+        for j in range(2):
+            (ar, ai), (br, bi) = left[i], right[j]
+            (cr, ci), (dr, di) = left[2 + i], right[2 + j]
+            out.append(
+                (
+                    (ar * br + ai * bi) + (cr * dr + ci * di),
+                    (ar * bi - ai * br) + (cr * di - ci * dr),
+                )
+            )
+    return out
+
+
+def scaled(er, ei, m):
+    return [(er * r - ei * i, er * i + ei * r) for r, i in m]
+
+
+def scaled_conj(er, ei, m):
+    return [(er * r + ei * i, er * i - ei * r) for r, i in m]
+
+
+def local_kernel(
+    degree_count,
+    together,
+    uvw_ref,
+    pair_ref,
+    dir_ref,
+    bright_ref,
+    seen_ref,
+    coeff_ref,
+    part_ref,
+    resid_ref,
+    jones,
+    with_b,
+    with_badj,
+    grads,
+    seen,
+    diffs,
+):
+    channels = bright_ref.shape[1]
+    stations = coeff_ref.shape[0]
+    pairs = uvw_ref.shape[1]
+    groups = channels // ROWS
+    tile = (ROWS, LANES)
+    f32 = jnp.float32
+    row = lax.broadcasted_iota(jnp.int32, tile, 0)
+    lane = lax.broadcasted_iota(jnp.int32, tile, 1)
+    span = max(channels - 1, 1)
+    xs = [(2.0 * (row + ROWS * g).astype(f32) - (channels - 1)) / span for g in range(groups)]
+    ratio = 1.0 + 0.25 * xs[0]
+    stride = 0.25 * 2.0 * ROWS / span
+
+    def block(ref, g, lead=()):
+        return [
+            tuple(
+                ref[(*lead, 2 * e + t, pl.ds(ROWS * g, ROWS), slice(None))] for t in range(2)
+            )
+            for e in range(4)
+        ]
+
+    for g in range(groups):
+        for comp in range(8):
+            seen[comp, pl.ds(ROWS * g, ROWS), :] = seen_ref[
+                pl.ds(8 * ROWS * g + comp, ROWS, stride=8), :
+            ]
+
+    def prepare(s, carry):
+        table = [
+            jnp.broadcast_to(coeff_ref[s, pl.ds(i, 1), :], tile) for i in range(8 * degree_count)
+        ]
+        for g in range(groups):
+            rows = pl.ds(ROWS * g, ROWS)
+            flat = []
+            for comp in range(8):
+                value = table[8 * (degree_count - 1) + comp]
+                for n in range(degree_count - 2, -1, -1):
+                    value = value * xs[g] + table[8 * n + comp]
+                flat.append(value)
+            j = [(flat[2 * e], flat[2 * e + 1]) for e in range(4)]
+            b = block(bright_ref, g)
+            a = times(j, b)
+            d = times_adj(j, b)
+            for e in range(4):
+                for t in range(2):
+                    jones[s, 2 * e + t, rows, :] = j[e][t]
+                    with_b[s, 2 * e + t, rows, :] = a[e][t]
+                    with_badj[s, 2 * e + t, rows, :] = d[e][t]
+                    grads[s, 2 * e + t, rows, :] = jnp.zeros(tile, f32)
+        return carry
+
+    lax.fori_loop(0, stations, prepare, 0)
+
+    l = jnp.broadcast_to(dir_ref[0:1, :], tile)
+    m = jnp.broadcast_to(dir_ref[1:2, :], tile)
+    depth = jnp.sqrt(1.0 - l * l - m * m) - 1.0
+
+    def predict(b):
+        p, q = pair_ref[0, b], pair_ref[1, b]
+        inner = uvw_ref[0, b] * l + uvw_ref[1, b] * m + uvw_ref[2, b] * depth
+        s, c = turn_sin_cos(ratio * inner)
+        step_s, step_c = turn_sin_cos(stride * inner)
+        er, ei = c, -s
+        here = lane == b
+        out = []
+        for g in range(groups):
+            if g:
+                er, ei = er * step_c + ei * step_s, ei * step_c - er * step_s
+            t = scaled(er, ei, block(with_b, g, (p,)))
+            model = times_adj(t, block(jones, g, (q,)))
+            rows = pl.ds(ROWS * g, ROWS)
+            diff = []
+            for e in range(4):
+                pieces = []
+                for k in range(2):
+                    comp = 2 * e + k
+                    term = model[e][k] - jnp.where(here, seen[comp, rows, :], 0.0)
+                    total = jnp.broadcast_to(jnp.sum(term, axis=1, keepdims=True), tile)
+                    pltpu.store(diffs.at[comp, rows, :], total, mask=here)
+                    pieces.append(total)
+                diff.append(tuple(pieces))
+            out.append((er, ei, t, diff))
+        return p, q, out
+
+    def deposit(state):
+        p, q, out = state
+        for g in range(groups):
+            rows = pl.ds(ROWS * g, ROWS)
+            er, ei, t, diff = out[g]
+            near = times(diff, scaled_conj(er, ei, block(with_badj, g, (q,))))
+            far = adj_times(diff, t)
+            for station, slope in ((p, near), (q, far)):
+                for e in range(4):
+                    for k in range(2):
+                        grads[station, 2 * e + k, rows, :] += slope[e][k]
+
+    def visit(i, carry):
+        last = predict(i * together)
+        for u in range(1, together):
+            state = predict(i * together + u)
+            deposit(last)
+            last = state
+        deposit(last)
+        return carry
+
+    lax.fori_loop(0, pairs // together, visit, 0)
+
+    def finish(s, carry):
+        for comp in range(8):
+            terms = [grads[s, comp, pl.ds(ROWS * g, ROWS), :] for g in range(groups)]
+            for n in range(degree_count):
+                if n:
+                    terms = [v * x for v, x in zip(terms, xs)]
+                part_ref[s, pl.ds(8 * n + comp, 1), :] = jnp.sum(
+                    sum(terms[1:], terms[0]), axis=0, keepdims=True
+                )
+        return carry
+
+    lax.fori_loop(0, stations, finish, 0)
+
+    for g in range(groups):
+        for comp in range(8):
+            resid_ref[pl.ds(8 * ROWS * g + comp, ROWS, stride=8), :] = -diffs[
+                comp, pl.ds(ROWS * g, ROWS), :
+            ]
+
+
+def gather(own, n):
+    vmem = pl.BlockSpec(memory_space=pltpu.VMEM)
+    return pl.pallas_call(
+        functools.partial(gather_kernel, n),
+        out_shape=jax.ShapeDtypeStruct((n, *own.shape), own.dtype),
+        in_specs=[vmem],
+        out_specs=vmem,
+        scratch_shapes=[pltpu.SemaphoreType.DMA((n,)), pltpu.SemaphoreType.DMA((n,))],
+        compiler_params=pltpu.CompilerParams(collective_id=1, has_side_effects=True),
+        name="gather_coefficients",
+    )(own)
+
+
+def scatter_sum(parts, n):
+    vmem = pl.BlockSpec(memory_space=pltpu.VMEM)
+    return pl.pallas_call(
+        functools.partial(scatter_sum_kernel, n),
+        out_shape=jax.ShapeDtypeStruct(parts.shape[1:], parts.dtype),
+        in_specs=[vmem],
+        out_specs=vmem,
+        scratch_shapes=[
+            pltpu.VMEM(parts.shape, parts.dtype),
+            pltpu.SemaphoreType.DMA((n,)),
+            pltpu.SemaphoreType.DMA((n,)),
+        ],
+        compiler_params=pltpu.CompilerParams(collective_id=2, has_side_effects=True),
+        name="sum_gradient",
+    )(parts)
+
+
+def compact_shards(uvw, directions, brightness, observed, coefficients, pair):
+    n = lax.axis_size("stn")
+    channels, dirs = brightness.shape[1:]
+    held, rows = coefficients.shape[:2]
+    pairs = uvw.shape[1]
+    table = gather(coefficients, n).reshape(n * held, rows, dirs)
+    vmem = pl.BlockSpec(memory_space=pltpu.VMEM)
+    smem = pl.BlockSpec(memory_space=pltpu.SMEM)
+    per_station = pltpu.VMEM((n * held, 8, channels, dirs), jnp.float32)
+    per_pair = pltpu.VMEM((8, channels, pairs), jnp.float32)
+    partial, residual = pl.pallas_call(
+        functools.partial(local_kernel, rows // 8, 4),
+        out_shape=(
+            jax.ShapeDtypeStruct(table.shape, jnp.float32),
+            jax.ShapeDtypeStruct((channels * 8, pairs), jnp.float32),
+        ),
+        in_specs=[smem, smem, vmem, vmem, vmem, vmem],
+        out_specs=(vmem, vmem),
+        scratch_shapes=[per_station] * 4 + [per_pair] * 2,
+        compiler_params=pltpu.CompilerParams(vmem_limit_bytes=VMEM_BUDGET),
+        name="predict_and_slope",
+    )(uvw, pair, directions, brightness, observed.reshape(channels * 8, pairs), table)
+    gradient = scatter_sum(partial.reshape(n, held, rows, dirs), n)
+    return gradient, residual.reshape(channels, 8, pairs)
+
+
+def shards(uvw, directions, brightness, observed, coefficients, pair):
+    channels, dirs = brightness.shape[1:]
+    stations = lax.axis_size("stn") * coefficients.shape[0]
+    fits = 4 * stations * 8 * channels * dirs * 4 <= VMEM_BUDGET // 2
+    if fits and dirs == LANES and uvw.shape[1] == LANES and channels % ROWS == 0:
+        return compact_shards(uvw, directions, brightness, observed, coefficients, pair)
+    return general_shards(uvw, directions, brightness, observed, coefficients, pair)
+
+
 def solution(mesh):
     placed = (
         P(None, ("grp", "stn")),

time: 411 us -> 60.6 us (0.15)
  local copies, waits for them, and re-layouts: 158 us -> 3.74 us
  other arithmetic: 124 us -> 0 us
  waiting for transfers between devices: 85.3 us -> 0 us
  Pallas kernels: 0 us -> 55.2 us
  blocking collectives: 24.4 us -> 0 us
  between operations: 14.8 us -> 0.72 us
    unnamed x2 -> x0, waiting for transfers between devices: 85.3 us -> none
    pallas_call x0 -> x3, Pallas kernels: none -> 55.2 us  [the longest x1 25.6 us: compact_shards(): pl.pallas_call(functools.partial(local_kernel, rows // 8, 4), out_shape=(...]
    mul x93 -> x0, local copies, waits for them, and re-layouts: 45.2 us -> none  [the longest x80 38.5 us: mat_product(): first_re = left_re[:, 0:1] * right_re[0:1] - left_im[:, 0:1] * right_im[0:1]]
    gather x8 -> x0, local copies, waits for them, and re-layouts: 40 us -> none  [the longest x4 20 us: visit_block(): jnp.take(jones_all, pick_near, axis=0)]
    add x21 -> x0, other arithmetic: 32.8 us -> none  [the longest x4 11.8 us: baseline_terms(): coh_re = bright_re * cosine + bright_im * sine_part]
    while x112 -> x0, local copies, waits for them, and re-layouts: 32.1 us -> none
    reduce_sum x8 -> x0, other arithmetic: 31.3 us -> none  [the longest x4 23.4 us: contract(): jnp.sum(grads * powers[degree][None, :, None, None], axis=1)]
    all_gather x1 -> x0, blocking collectives: 24.4 us -> none  [shards(): lax.all_gather(coefficients, 'stn', axis=0, tiled=True)]
  transfers between devices with their start and end apart: 1 -> 0, of which waited for: 1 -> 0; matrix products, arithmetic and copies ran while one was open for 0% -> 0% of each run, Pallas kernels for 0% -> 0%
where the time goes in v1:
time: 60.6 us; the launch traced here: 59.7 us
  Pallas kernels  55.2 us (91%)
  local copies, waits for them, and re-layouts  3.74 us (6%)
  between operations  0.72 us (1%)
    pallas_call x1, Pallas kernels, compact_shards(): pl.pallas_call(functools.partial(local_kernel, rows // 8, 4), out_shape=(...  25.6 us
    pallas_call x1, Pallas kernels, scatter_sum(): pl.pallas_call(functools.partial(scatter_sum_kernel, n), out_shape=jax.Sh...  14.9 us
    pallas_call x1, Pallas kernels, gather(): pl.pallas_call(functools.partial(gather_kernel, n), out_shape=jax.ShapeDt...  14.8 us
    unnamed x15, local copies, waits for them, and re-layouts  3.74 us

profile of v1, /device:TPU:0, one launch (start us, length us, event | category | flops | bytes accessed | tf_op | source)
XLA Modules:
  0.0 59.7 jit_solution(7533833196525889131)
XLA Ops:
  0.6 0.0 copy-start.2
  0.6 0.0 copy-start.3
  0.7 0.0 copy-start.4
  0.7 0.0 copy-start.6
  0.7 14.8 %gather_coefficients.1 = f32[16,2,24,128]{3,2,1,0:T(8,128)} custom-call(f32[2,24,128]{2,1,0:T(8,128)} %own_ref.1), custom_call_target="tpu_custom_call" | custom-call | tf_op jit(solution)/shard_map/gather_coefficients/pallas_call | solution.py:441
  15.4 0.0 copy-start.5
  15.5 0.0 copy-done.2
  15.5 0.0 copy-done.3
  15.5 0.0 copy-done.4
  15.5 0.0 copy-done.6
  15.5 0.6 %copy-done.5 = s32[2,128]{1,0:T(2,128)S(1)} copy-done((s32[2,128]{1,0:T(2,128)S(1)}, s32[2,128]{1,0:T(2,128)}, u32[]{:S(2)}) %copy-start.5) | copy-done | bytes 1048
  16.1 0.0 copy-start
  16.1 1.0 %copy-done = f32[16,2,24,128]{3,2,1,0:T(8,128)S(1)} copy-done((f32[16,2,24,128]{3,2,1,0:T(8,128)S(1)}, f32[16,2,24,128]{3,2,1,0:T(8,128)}, u32[]{:S(2)}) %copy-start) | copy-done | bytes 393240
  17.1 25.6 %predict_and_slope.1 = (f32[32,24,128]{2,1,0:T(8,128)S(1)}, f32[256,128]{1,0:T(8,128)}) custom-call(f32[3,128]{1,0:T(4,128)S(1)} %copy-done.4, s32[2,128]{1,0:T(2,128)S(1)} %copy-done.5, f32[2,128]{1,0:T(2,128)S(1)} %copy-done.6, f32[8,32,128]{2,1,0:T(8,128)S(1)} %copy-done.2, f32[256,128]{1,0:T(8,128)S(1)} %bitcast.6, f32[32,24,128]{2,1,0:T(8,128)S(1)} %bitcast.4), custom_call_target="tpu_custom_call" | custom-call | tf_op jit(solution)/shard_map/predict_and_slope/pallas_call | solution.py:479
  42.7 0.0 copy-start.1
  42.7 0.7 %copy-done.1 = f32[32,24,128]{2,1,0:T(8,128)} copy-done((f32[32,24,128]{2,1,0:T(8,128)}, f32[32,24,128]{2,1,0:T(8,128)S(1)}, u32[]{:S(2)}) %copy-start.1) | copy-done | bytes 393240
  43.4 14.9 %sum_gradient.1 = f32[2,24,128]{2,1,0:T(8,128)} custom-call(f32[16,2,24,128]{3,2,1,0:T(8,128)} %bitcast.5), custom_call_target="tpu_custom_call" | custom-call | tf_op jit(solution)/shard_map/sum_gradient/pallas_call | solution.py:454
  58.3 1.3 %copy.9 = f32[2,24,128]{2,1,0:T(8,128)} copy(f32[2,24,128]{2,1,0:T(8,128)} %sum_gradient.1) | data formatting | bytes 49152
Async XLA Ops:
  0.6 14.8 %copy-start.2 = (f32[8,32,128]{2,1,0:T(8,128)S(1)}, f32[8,32,128]{2,1,0:T(8,128)}, u32[]{:S(2)}) copy-start(f32[8,32,128]{2,1,0:T(8,128)} %bright_ref.1) | copy-start | bytes 393220
  0.6 14.8 %copy-start.3 = (f32[32,8,128]{2,1,0:T(8,128)S(1)}, f32[32,8,128]{2,1,0:T(8,128)}, u32[]{:S(2)}) copy-start(f32[32,8,128]{2,1,0:T(8,128)} %param.9) | copy-start | bytes 393220
  0.7 14.8 %copy-start.4 = (f32[3,128]{1,0:T(4,128)S(1)}, f32[3,128]{1,0:T(4,128)}, u32[]{:S(2)}) copy-start(f32[3,128]{1,0:T(4,128)} %uvw_ref.1) | copy-start | bytes 4612
  0.7 14.8 %copy-start.6 = (f32[2,128]{1,0:T(2,128)S(1)}, f32[2,128]{1,0:T(2,128)}, u32[]{:S(2)}) copy-start(f32[2,128]{1,0:T(2,128)} %dir_ref.1) | copy-start | bytes 3076
  15.4 0.7 %copy-start.5 = (s32[2,128]{1,0:T(2,128)S(1)}, s32[2,128]{1,0:T(2,128)}, u32[]{:S(2)}) copy-start(s32[2,128]{1,0:T(2,128)} %pair_ref.1) | copy-start | bytes 3076
  16.1 1.0 %copy-start = (f32[16,2,24,128]{3,2,1,0:T(8,128)S(1)}, f32[16,2,24,128]{3,2,1,0:T(8,128)}, u32[]{:S(2)}) copy-start(f32[16,2,24,128]{3,2,1,0:T(8,128)} %gather_coefficients.1) | copy-start | bytes 1179652
  42.7 0.7 %copy-start.1 = (f32[32,24,128]{2,1,0:T(8,128)}, f32[32,24,128]{2,1,0:T(8,128)S(1)}, u32[]{:S(2)}) copy-start(f32[32,24,128]{2,1,0:T(8,128)S(1)} %get-tuple-element.4) | copy-start | bytes 1179652

commit v2 on v1

--- a/solution.py
+++ b/solution.py
@@ -171,58 +171,127 @@
     return (gradient, residual)
 
 
-def greet(n):
+def place(n):
+    cores = 2 if n % 2 == 0 else 1
+    columns = 2 if n % (2 * cores) == 0 else 1
+    depth = n // (cores * columns)
     me = lax.axis_index("stn")
-    barrier = pltpu.get_barrier_semaphore()
-    for d in range(1, n):
-        pl.semaphore_signal(
-            barrier, inc=1, device_id={"stn": lax.rem(me + d, n)}, device_id_type=MESH
-        )
-    pl.semaphore_wait(barrier, n - 1)
-    return me
-
-
-def gather_kernel(n, own_ref, all_ref, send_sem, recv_sem):
-    me = greet(n)
-    copies = []
-    for d in range(1, n):
+    z, rest = lax.div(me, cores * columns), lax.rem(me, cores * columns)
+    return depth, columns, cores, z, lax.div(rest, cores), lax.rem(rest, cores)
+
+
+class Hops:
+    def __init__(self, n, send_sem, recv_sem):
+        self.depth, self.columns, self.cores, self.z, self.x, self.c = place(n)
+        self.send_sem, self.recv_sem = send_sem, recv_sem
+        self.copies = {}
+
+    def index(self, dz, dx, dc):
+        z = lax.rem(self.z + dz + self.depth, self.depth)
+        x = 1 - self.x if dx else self.x
+        c = 1 - self.c if dc else self.c
+        return (z * self.columns + x) * self.cores + c
+
+    def greet(self):
+        barrier = pltpu.get_barrier_semaphore()
+        peers = [(d, 0, 0) for d in range(1, self.depth)]
+        peers += [(0, 1, 0)] * (self.columns > 1) + [(0, 0, 1)] * (self.cores > 1)
+        for peer in peers:
+            pl.semaphore_signal(
+                barrier, inc=1, device_id={"stn": self.index(*peer)}, device_id_type=MESH
+            )
+        pl.semaphore_wait(barrier, len(peers))
+
+    def send(self, key, peer, src, dst):
+        number = len(self.copies)
         copy = pltpu.make_async_remote_copy(
-            src_ref=own_ref,
-            dst_ref=all_ref.at[me],
-            send_sem=send_sem.at[d],
-            recv_sem=recv_sem.at[d],
-            device_id={"stn": lax.rem(me + d, n)},
+            src_ref=src,
+            dst_ref=dst,
+            send_sem=self.send_sem.at[number],
+            recv_sem=self.recv_sem.at[number],
+            device_id={"stn": self.index(*peer)},
             device_id_type=MESH,
         )
         copy.start()
-        copies.append(copy)
-    all_ref[me] = own_ref[...]
-    for copy in copies:
-        copy.wait()
-
-
-def scatter_sum_kernel(n, part_ref, sum_ref, held, send_sem, recv_sem):
-    me = greet(n)
-    copies = []
-    for d in range(1, n):
-        peer = lax.rem(me + d, n)
-        copy = pltpu.make_async_remote_copy(
-            src_ref=part_ref.at[peer],
-            dst_ref=held.at[d],
-            send_sem=send_sem.at[d],
-            recv_sem=recv_sem.at[d],
-            device_id={"stn": peer},
-            device_id_type=MESH,
+        self.copies[key] = copy
+
+    def arrived(self, key):
+        self.copies[key].wait_recv()
+
+    def settle(self):
+        for copy in self.copies.values():
+            copy.wait_send()
+
+
+def gather_kernel(n, own_ref, all_ref, held, send_sem, recv_sem, out_sem):
+    hops = Hops(n, send_sem, recv_sem)
+    outs = []
+
+    def keep(src, slot):
+        out = pltpu.make_async_copy(src, all_ref.at[slot], out_sem.at[len(outs)])
+        out.start()
+        outs.append(out)
+
+    me = hops.index(0, 0, 0)
+    mine = held.at[me]
+    hops.greet()
+    for d in range(1, hops.depth):
+        hops.send(("z", d), (d, 0, 0), own_ref, mine)
+    hops.send(("x", 0), (0, 1, 0), own_ref, mine)
+    hops.send(("c", 0, 0), (0, 0, 1), own_ref, mine)
+    keep(own_ref, me)
+    for d in range(1, hops.depth):
+        hops.arrived(("z", d))
+        slot = hops.index(-d, 0, 0)
+        hops.send(("x", d), (0, 1, 0), held.at[slot], held.at[slot])
+        hops.send(("c", d, 0), (0, 0, 1), held.at[slot], held.at[slot])
+        keep(held.at[slot], slot)
+    for d in range(hops.depth):
+        hops.arrived(("x", d))
+        slot = hops.index(-d, 1, 0)
+        hops.send(("c", d, 1), (0, 0, 1), held.at[slot], held.at[slot])
+        keep(held.at[slot], slot)
+    for dx in range(2):
+        for d in range(hops.depth):
+            hops.arrived(("c", d, dx))
+            slot = hops.index(-d, dx, 1)
+            keep(held.at[slot], slot)
+    for out in outs:
+        out.wait()
+    hops.settle()
+
+
+def scatter_sum_kernel(n, part_ref, sum_ref, own, from_c, from_x, from_z, send_sem, recv_sem, in_sem):
+    hops = Hops(n, send_sem, recv_sem)
+    order = [(d, dx) for dx in (1, 0) for d in [*range(1, hops.depth), 0]]
+    ins = {}
+    for k, (d, dx) in enumerate(order):
+        ins[d, dx] = pltpu.make_async_copy(
+            part_ref.at[hops.index(d, dx, 0)], own.at[dx, d], in_sem.at[k]
         )
-        copy.start()
-        copies.append(copy)
-    total = part_ref[me]
-    for d, copy in enumerate(copies, 1):
-        copy.wait_recv()
-        total = total + held[d]
+        ins[d, dx].start()
+    hops.greet()
+    for d, dx in order:
+        hops.send(
+            ("c", d, dx), (0, 0, 1), part_ref.at[hops.index(d, dx, 1)], from_c.at[dx, d]
+        )
+    for d, dx in order:
+        ins[d, dx].wait()
+        hops.arrived(("c", d, dx))
+        if dx:
+            own[dx, d] = own[dx, d] + from_c[dx, d]
+            hops.send(("x", d), (0, 1, 0), own.at[dx, d], from_x.at[d])
+            continue
+        hops.arrived(("x", d))
+        total = own[dx, d] + from_c[dx, d] + from_x[d]
+        if d:
+            own[dx, d] = total
+            hops.send(("z", d), (d, 0, 0), own.at[dx, d], from_z.at[d])
+    for d in range(1, hops.depth):
+        hops.arrived(("z", d))
+        total = total + from_z[d]
     sum_ref[...] = total
-    for copy in copies:
-        copy.wait_send()
+    hops.settle()
 
 
 def turn_sin_cos(turns):
@@ -295,22 +364,46 @@
     degree_count,
     together,
     uvw_ref,
-    pair_ref,
+    pair_hbm,
     dir_ref,
     bright_ref,
     seen_ref,
+    coeff_hbm,
+    part_hbm,
+    resid_ref,
+    pair_ref,
     coeff_ref,
     part_ref,
-    resid_ref,
     jones,
     with_b,
     with_badj,
     grads,
     seen,
     diffs,
+    pair_sem,
+    table_sem,
 ):
     channels = bright_ref.shape[1]
     stations = coeff_ref.shape[0]
+    chunk = stations // table_sem.shape[0]
+
+    def span_of(s):
+        return pl.ds(pl.multiple_of(lax.div(s, chunk) * chunk, chunk), chunk)
+
+    def table_in(s):
+        return pltpu.make_async_copy(
+            coeff_hbm.at[span_of(s)], coeff_ref.at[span_of(s)], table_sem.at[lax.div(s, chunk)]
+        )
+
+    def part_out(s):
+        return pltpu.make_async_copy(
+            part_ref.at[span_of(s)], part_hbm.at[span_of(s)], table_sem.at[lax.div(s, chunk)]
+        )
+
+    for k in range(table_sem.shape[0]):
+        table_in(k * chunk).start()
+    pair_in = pltpu.make_async_copy(pair_hbm, pair_ref, pair_sem)
+    pair_in.start()
     pairs = uvw_ref.shape[1]
     groups = channels // ROWS
     tile = (ROWS, LANES)
@@ -337,6 +430,10 @@
             ]
 
     def prepare(s, carry):
+        @pl.when(lax.rem(s, chunk) == 0)
+        def _():
+            table_in(s).wait()
+
         table = [
             jnp.broadcast_to(coeff_ref[s, pl.ds(i, 1), :], tile) for i in range(8 * degree_count)
         ]
@@ -361,6 +458,7 @@
         return carry
 
     lax.fori_loop(0, stations, prepare, 0)
+    pair_in.wait()
 
     l = jnp.broadcast_to(dir_ref[0:1, :], tile)
     m = jnp.broadcast_to(dir_ref[1:2, :], tile)
@@ -425,6 +523,11 @@
                 part_ref[s, pl.ds(8 * n + comp, 1), :] = jnp.sum(
                     sum(terms[1:], terms[0]), axis=0, keepdims=True
                 )
+
+        @pl.when(lax.rem(s, chunk) == chunk - 1)
+        def _():
+            part_out(s).start()
+
         return carry
 
     lax.fori_loop(0, stations, finish, 0)
@@ -434,30 +537,40 @@
             resid_ref[pl.ds(8 * ROWS * g + comp, ROWS, stride=8), :] = -diffs[
                 comp, pl.ds(ROWS * g, ROWS), :
             ]
+    for k in range(table_sem.shape[0]):
+        part_out(k * chunk).wait()
 
 
 def gather(own, n):
-    vmem = pl.BlockSpec(memory_space=pltpu.VMEM)
     return pl.pallas_call(
         functools.partial(gather_kernel, n),
         out_shape=jax.ShapeDtypeStruct((n, *own.shape), own.dtype),
-        in_specs=[vmem],
-        out_specs=vmem,
-        scratch_shapes=[pltpu.SemaphoreType.DMA((n,)), pltpu.SemaphoreType.DMA((n,))],
+        in_specs=[pl.BlockSpec(memory_space=pltpu.VMEM)],
+        out_specs=pl.BlockSpec(memory_space=pl.ANY),
+        scratch_shapes=[
+            pltpu.VMEM((n, *own.shape), own.dtype),
+            pltpu.SemaphoreType.DMA((n,)),
+            pltpu.SemaphoreType.DMA((n,)),
+            pltpu.SemaphoreType.DMA((n,)),
+        ],
         compiler_params=pltpu.CompilerParams(collective_id=1, has_side_effects=True),
         name="gather_coefficients",
     )(own)
 
 
 def scatter_sum(parts, n):
-    vmem = pl.BlockSpec(memory_space=pltpu.VMEM)
+    piece = parts.shape[1:]
     return pl.pallas_call(
         functools.partial(scatter_sum_kernel, n),
-        out_shape=jax.ShapeDtypeStruct(parts.shape[1:], parts.dtype),
-        in_specs=[vmem],
-        out_specs=vmem,
+        out_shape=jax.ShapeDtypeStruct(piece, parts.dtype),
+        in_specs=[pl.BlockSpec(memory_space=pl.ANY)],
+        out_specs=pl.BlockSpec(memory_space=pltpu.VMEM),
         scratch_shapes=[
-            pltpu.VMEM(parts.shape, parts.dtype),
+            pltpu.VMEM((2, n // 4, *piece), parts.dtype),
+            pltpu.VMEM((2, n // 4, *piece), parts.dtype),
+            pltpu.VMEM((n // 4, *piece), parts.dtype),
+            pltpu.VMEM((n // 4, *piece), parts.dtype),
+            pltpu.SemaphoreType.DMA((n,)),
             pltpu.SemaphoreType.DMA((n,)),
             pltpu.SemaphoreType.DMA((n,)),
         ],
@@ -473,6 +586,7 @@
     pairs = uvw.shape[1]
     table = gather(coefficients, n).reshape(n * held, rows, dirs)
     vmem = pl.BlockSpec(memory_space=pltpu.VMEM)
+    away = pl.BlockSpec(memory_space=pl.ANY)
     smem = pl.BlockSpec(memory_space=pltpu.SMEM)
     per_station = pltpu.VMEM((n * held, 8, channels, dirs), jnp.float32)
     per_pair = pltpu.VMEM((8, channels, pairs), jnp.float32)
@@ -482,9 +596,13 @@
             jax.ShapeDtypeStruct(table.shape, jnp.float32),
             jax.ShapeDtypeStruct((channels * 8, pairs), jnp.float32),
         ),
-        in_specs=[smem, smem, vmem, vmem, vmem, vmem],
-        out_specs=(vmem, vmem),
-        scratch_shapes=[per_station] * 4 + [per_pair] * 2,
+        in_specs=[smem, away, vmem, vmem, vmem, away],
+        out_specs=(away, vmem),
+        scratch_shapes=[pltpu.SMEM(pair.shape, pair.dtype)]
+        + [pltpu.VMEM(table.shape, jnp.float32)] * 2
+        + [per_station] * 4
+        + [per_pair] * 2
+        + [pltpu.SemaphoreType.DMA, pltpu.SemaphoreType.DMA((4,))],
         compiler_params=pltpu.CompilerParams(vmem_limit_bytes=VMEM_BUDGET),
         name="predict_and_slope",
     )(uvw, pair, directions, brightness, observed.reshape(channels * 8, pairs), table)
@@ -495,7 +613,7 @@
 def shards(uvw, directions, brightness, observed, coefficients, pair):
     channels, dirs = brightness.shape[1:]
     stations = lax.axis_size("stn") * coefficients.shape[0]
-    fits = 4 * stations * 8 * channels * dirs * 4 <= VMEM_BUDGET // 2
+    fits = lax.axis_size("stn") % 4 == 0 and 4 * stations * 8 * channels * dirs * 4 <= VMEM_BUDGET // 2
     if fits and dirs == LANES and uvw.shape[1] == LANES and channels % ROWS == 0:
         return compact_shards(uvw, directions, brightness, observed, coefficients, pair)
     return general_shards(uvw, directions, brightness, observed, coefficients, pair)

time: 60.6 us -> 56.7 us (0.936); the launches traced: 59.7 us -> 56.4 us
  Pallas kernels: 55.2 us -> 52 us
    pallas_call x1, Pallas kernels: 14.9 us -> 11.5 us  [scatter_sum(): pl.pallas_call(functools.partial(scatter_sum_kernel, n), out_shape=jax.Sh...]
    pallas_call x1, Pallas kernels: 25.6 us -> 26.9 us  [compact_shards(): pl.pallas_call(functools.partial(local_kernel, rows // 8, 4), out_shape=(...]
    pallas_call x1, Pallas kernels: 14.8 us -> 13.6 us  [gather(): pl.pallas_call(functools.partial(gather_kernel, n), out_shape=jax.ShapeDt...]
where the time goes in v2:
time: 56.7 us; the launch traced here: 56.4 us
  Pallas kernels  52 us (92%)
  local copies, waits for them, and re-layouts  3.73 us (7%)
  between operations  0.74 us (1%)
    pallas_call x1, Pallas kernels, compact_shards(): pl.pallas_call(functools.partial(local_kernel, rows // 8, 4), out_shape=(...  26.9 us
    pallas_call x1, Pallas kernels, gather(): pl.pallas_call(functools.partial(gather_kernel, n), out_shape=jax.ShapeDt...  13.6 us
    pallas_call x1, Pallas kernels, scatter_sum(): pl.pallas_call(functools.partial(scatter_sum_kernel, n), out_shape=jax.Sh...  11.5 us
    unnamed x15, local copies, waits for them, and re-layouts  3.73 us

profile of v2, /device:TPU:0, one launch (start us, length us, event | category | flops | bytes accessed | tf_op | source)
XLA Modules:
  0.0 56.4 jit_solution(14108595786075354476)
XLA Ops:
  0.6 0.0 copy-start.2
  0.6 0.0 copy-start.3
  0.7 0.0 copy-start.4
  0.7 0.0 copy-start.6
  0.7 13.6 %gather_coefficients.1 = f32[16,2,24,128]{3,2,1,0:T(8,128)} custom-call(f32[2,24,128]{2,1,0:T(8,128)} %own_ref.1), custom_call_target="tpu_custom_call" | custom-call | tf_op jit(solution)/shard_map/gather_coefficients/pallas_call | solution.py:545
  14.3 0.0 copy-start.5
  14.3 0.0 copy-done.2
  14.3 0.0 copy-done.3
  14.3 0.0 copy-done.4
  14.3 0.0 copy-done.6
  14.3 0.6 %copy-done.5 = s32[2,128]{1,0:T(2,128)S(1)} copy-done((s32[2,128]{1,0:T(2,128)S(1)}, s32[2,128]{1,0:T(2,128)}, u32[]{:S(2)}) %copy-start.5) | copy-done | bytes 1048
  15.0 0.0 copy-start
  15.0 1.0 %copy-done = f32[16,2,24,128]{3,2,1,0:T(8,128)S(1)} copy-done((f32[16,2,24,128]{3,2,1,0:T(8,128)S(1)}, f32[16,2,24,128]{3,2,1,0:T(8,128)}, u32[]{:S(2)}) %copy-start) | copy-done | bytes 393240
  16.0 26.9 %predict_and_slope.1 = (f32[32,24,128]{2,1,0:T(8,128)S(1)}, f32[256,128]{1,0:T(8,128)}) custom-call(f32[3,128]{1,0:T(4,128)S(1)} %copy-done.4, s32[2,128]{1,0:T(2,128)S(1)} %copy-done.5, f32[2,128]{1,0:T(2,128)S(1)} %copy-done.6, f32[8,32,128]{2,1,0:T(8,128)S(1)} %copy-done.2, f32[256,128]{1,0:T(8,128)S(1)} %bitcast.6, f32[32,24,128]{2,1,0:T(8,128)S(1)} %bitcast.4), custom_call_target="tpu_custom_call" | custom-call | tf_op jit(solution)/shard_map/predict_and_slope/pallas_call | solution.py:593
  42.8 0.0 copy-start.1
  42.8 0.7 %copy-done.1 = f32[32,24,128]{2,1,0:T(8,128)} copy-done((f32[32,24,128]{2,1,0:T(8,128)}, f32[32,24,128]{2,1,0:T(8,128)S(1)}, u32[]{:S(2)}) %copy-start.1) | copy-done | bytes 393240
  43.6 11.5 %sum_gradient.1 = f32[2,24,128]{2,1,0:T(8,128)} custom-call(f32[16,2,24,128]{3,2,1,0:T(8,128)} %bitcast.5), custom_call_target="tpu_custom_call" | custom-call | tf_op jit(solution)/shard_map/sum_gradient/pallas_call | solution.py:563
  55.1 1.3 %copy.9 = f32[2,24,128]{2,1,0:T(8,128)} copy(f32[2,24,128]{2,1,0:T(8,128)} %sum_gradient.1) | data formatting | bytes 49152
Async XLA Ops:
  0.6 13.7 %copy-start.2 = (f32[8,32,128]{2,1,0:T(8,128)S(1)}, f32[8,32,128]{2,1,0:T(8,128)}, u32[]{:S(2)}) copy-start(f32[8,32,128]{2,1,0:T(8,128)} %bright_ref.1) | copy-start | bytes 393220
  0.6 13.7 %copy-start.3 = (f32[32,8,128]{2,1,0:T(8,128)S(1)}, f32[32,8,128]{2,1,0:T(8,128)}, u32[]{:S(2)}) copy-start(f32[32,8,128]{2,1,0:T(8,128)} %param.9) | copy-start | bytes 393220
  0.7 13.7 %copy-start.4 = (f32[3,128]{1,0:T(4,128)S(1)}, f32[3,128]{1,0:T(4,128)}, u32[]{:S(2)}) copy-start(f32[3,128]{1,0:T(4,128)} %uvw_ref.1) | copy-start | bytes 4612
  0.7 13.7 %copy-start.6 = (f32[2,128]{1,0:T(2,128)S(1)}, f32[2,128]{1,0:T(2,128)}, u32[]{:S(2)}) copy-start(f32[2,128]{1,0:T(2,128)} %dir_ref.1) | copy-start | bytes 3076
  14.3 0.7 %copy-start.5 = (s32[2,128]{1,0:T(2,128)S(1)}, s32[2,128]{1,0:T(2,128)}, u32[]{:S(2)}) copy-start(s32[2,128]{1,0:T(2,128)} %pair_hbm.1) | copy-start | bytes 3076
  15.0 1.0 %copy-start = (f32[16,2,24,128]{3,2,1,0:T(8,128)S(1)}, f32[16,2,24,128]{3,2,1,0:T(8,128)}, u32[]{:S(2)}) copy-start(f32[16,2,24,128]{3,2,1,0:T(8,128)} %gather_coefficients.1) | copy-start | bytes 1179652
  42.8 0.7 %copy-start.1 = (f32[32,24,128]{2,1,0:T(8,128)}, f32[32,24,128]{2,1,0:T(8,128)S(1)}, u32[]{:S(2)}) copy-start(f32[32,24,128]{2,1,0:T(8,128)S(1)} %get-tuple-element.4) | copy-start | bytes 1179652

commit v3 on v2

--- a/solution.py
+++ b/solution.py
@@ -307,57 +307,34 @@
     return 2.0 * (s * c), 1.0 - 2.0 * (s * s)
 
 
-def times(left, right):
-    out = []
-    for i in range(2):
-        for j in range(2):
-            (ar, ai), (br, bi) = left[2 * i], right[j]
-            (cr, ci), (dr, di) = left[2 * i + 1], right[2 + j]
-            out.append(
-                (
-                    (ar * br - ai * bi) + (cr * dr - ci * di),
-                    (ar * bi + ai * br) + (cr * di + ci * dr),
-                )
-            )
-    return out
-
-
-def times_adj(left, right):
-    out = []
-    for i in range(2):
-        for j in range(2):
-            (ar, ai), (br, bi) = left[2 * i], right[2 * j]
-            (cr, ci), (dr, di) = left[2 * i + 1], right[2 * j + 1]
-            out.append(
-                (
-                    (ar * br + ai * bi) + (cr * dr + ci * di),
-                    (ai * br - ar * bi) + (ci * dr - cr * di),
-                )
-            )
-    return out
-
-
-def adj_times(left, right):
-    out = []
-    for i in range(2):
-        for j in range(2):
-            (ar, ai), (br, bi) = left[i], right[j]
-            (cr, ci), (dr, di) = left[2 + i], right[2 + j]
-            out.append(
-                (
-                    (ar * br + ai * bi) + (cr * dr + ci * di),
-                    (ar * bi - ai * br) + (cr * di - ci * dr),
-                )
-            )
-    return out
-
-
 def scaled(er, ei, m):
     return [(er * r - ei * i, er * i + ei * r) for r, i in m]
 
 
 def scaled_conj(er, ei, m):
     return [(er * r + ei * i, er * i - ei * r) for r, i in m]
+
+
+def real_times(left, right):
+    return [
+        left[2 * i] * right[j] + left[2 * i + 1] * right[2 + j] for i in range(2) for j in range(2)
+    ]
+
+
+def flipped(m):
+    return [m[0], m[2], m[1], m[3]]
+
+
+def both(m):
+    return [r + i for r, i in m]
+
+
+def plus(a, b):
+    return [x + y for x, y in zip(a, b)]
+
+
+def minus(a, b):
+    return [x - y for x, y in zip(a, b)]
 
 
 def local_kernel(
@@ -380,6 +357,9 @@
     grads,
     seen,
     diffs,
+    forms,
+    turns,
+    steps,
     pair_sem,
     table_sem,
 ):
@@ -428,6 +408,9 @@
             seen[comp, pl.ds(ROWS * g, ROWS), :] = seen_ref[
                 pl.ds(8 * ROWS * g + comp, ROWS, stride=8), :
             ]
+        for e, (re, im) in enumerate(block(bright_ref, g)):
+            forms[e, pl.ds(ROWS * g, ROWS), :] = re + im
+            forms[4 + e, pl.ds(ROWS * g, ROWS), :] = re - im
 
     def prepare(s, carry):
         @pl.when(lax.rem(s, chunk) == 0)
@@ -445,16 +428,29 @@
                 for n in range(degree_count - 2, -1, -1):
                     value = value * xs[g] + table[8 * n + comp]
                 flat.append(value)
-            j = [(flat[2 * e], flat[2 * e + 1]) for e in range(4)]
-            b = block(bright_ref, g)
-            a = times(j, b)
-            d = times_adj(j, b)
+            jr, ji = flat[0::2], flat[1::2]
+            js = plus(jr, ji)
+            br, bi = [bright_ref[2 * e, rows, :] for e in range(4)], [
+                bright_ref[2 * e + 1, rows, :] for e in range(4)
+            ]
+            bs, bd = [forms[e, rows, :] for e in range(4)], [
+                forms[4 + e, rows, :] for e in range(4)
+            ]
+            common = real_times(js, br)
+            a = (minus(common, real_times(ji, bs)), minus(common, real_times(jr, bd)))
+            common = real_times(js, flipped(br))
+            d = (
+                minus(common, real_times(ji, flipped(bd))),
+                minus(common, real_times(jr, flipped(bs))),
+            )
+            jd = minus(jr, ji)
             for e in range(4):
                 for t in range(2):
-                    jones[s, 2 * e + t, rows, :] = j[e][t]
-                    with_b[s, 2 * e + t, rows, :] = a[e][t]
-                    with_badj[s, 2 * e + t, rows, :] = d[e][t]
-                    grads[s, 2 * e + t, rows, :] = jnp.zeros(tile, f32)
+                    with_b[s, 2 * e + t, rows, :] = a[t][e]
+                    with_badj[s, 2 * e + t, rows, :] = d[t][e]
+                for t, form in enumerate((jr, js, jd)):
+                    jones[s, 4 * t + e, rows, :] = form[e]
+                    grads[s, 4 * t + e, rows, :] = jnp.zeros(tile, f32)
         return carry
 
     lax.fori_loop(0, stations, prepare, 0)
@@ -464,44 +460,74 @@
     m = jnp.broadcast_to(dir_ref[1:2, :], tile)
     depth = jnp.sqrt(1.0 - l * l - m * m) - 1.0
 
+    def measure(b, carry):
+        inner = uvw_ref[0, b] * l + uvw_ref[1, b] * m + uvw_ref[2, b] * depth
+        turns[pl.ds(b, 1), :] = inner[0:1, :]
+        return carry
+
+    lax.fori_loop(0, pairs, measure, 0, unroll=8)
+
+    def step_of(i, carry):
+        some = pl.ds(pl.multiple_of(i * ROWS, ROWS), ROWS)
+        s, c = turn_sin_cos(stride * turns[some, :])
+        steps[0, some, :] = s
+        steps[1, some, :] = c
+        return carry
+
+    lax.fori_loop(0, pairs // ROWS, step_of, 0)
+
     def predict(b):
         p, q = pair_ref[0, b], pair_ref[1, b]
-        inner = uvw_ref[0, b] * l + uvw_ref[1, b] * m + uvw_ref[2, b] * depth
-        s, c = turn_sin_cos(ratio * inner)
-        step_s, step_c = turn_sin_cos(stride * inner)
+        s, c = turn_sin_cos(ratio * jnp.broadcast_to(turns[pl.ds(b, 1), :], tile))
+        step_s = jnp.broadcast_to(steps[0, pl.ds(b, 1), :], tile)
+        step_c = jnp.broadcast_to(steps[1, pl.ds(b, 1), :], tile)
         er, ei = c, -s
         here = lane == b
         out = []
         for g in range(groups):
+            rows = pl.ds(ROWS * g, ROWS)
             if g:
                 er, ei = er * step_c + ei * step_s, ei * step_c - er * step_s
             t = scaled(er, ei, block(with_b, g, (p,)))
-            model = times_adj(t, block(jones, g, (q,)))
-            rows = pl.ds(ROWS * g, ROWS)
-            diff = []
+            tr, ti = [v[0] for v in t], [v[1] for v in t]
+            ts = plus(tr, ti)
+            jr, js, jd = [
+                flipped([jones[q, 4 * k + e, rows, :] for e in range(4)]) for k in range(3)
+            ]
+            common = real_times(ts, jr)
+            model = (minus(common, real_times(ti, jd)), minus(common, real_times(tr, js)))
+            diff = ([], [])
             for e in range(4):
-                pieces = []
                 for k in range(2):
                     comp = 2 * e + k
-                    term = model[e][k] - jnp.where(here, seen[comp, rows, :], 0.0)
+                    term = model[k][e] - jnp.where(here, seen[comp, rows, :], 0.0)
                     total = jnp.broadcast_to(jnp.sum(term, axis=1, keepdims=True), tile)
                     pltpu.store(diffs.at[comp, rows, :], total, mask=here)
-                    pieces.append(total)
-                diff.append(tuple(pieces))
-            out.append((er, ei, t, diff))
+                    diff[k].append(total)
+            out.append((er, ei, tr, ti, ts, diff))
         return p, q, out
 
     def deposit(state):
         p, q, out = state
         for g in range(groups):
             rows = pl.ds(ROWS * g, ROWS)
-            er, ei, t, diff = out[g]
-            near = times(diff, scaled_conj(er, ei, block(with_badj, g, (q,))))
-            far = adj_times(diff, t)
-            for station, slope in ((p, near), (q, far)):
+            er, ei, tr, ti, ts, (rr, ri) = out[g]
+            u = scaled_conj(er, ei, block(with_badj, g, (q,)))
+            ur, ui = [v[0] for v in u], [v[1] for v in u]
+            rp, rm = plus(rr, ri), minus(ri, rr)
+            near = (real_times(rr, both(u)), real_times(rp, ui), real_times(rm, ur))
+            for k in range(3):
                 for e in range(4):
-                    for k in range(2):
-                        grads[station, 2 * e + k, rows, :] += slope[e][k]
+                    grads[p, 4 * k + e, rows, :] += near[k][e]
+            far = (
+                real_times(flipped(rr), ts),
+                real_times(flipped(rm), ti),
+                real_times(flipped(rp), tr),
+            )
+            for e in range(4):
+                grads[q, e, rows, :] += far[0][e]
+                grads[q, 4 + e, rows, :] -= far[1][e]
+                grads[q, 8 + e, rows, :] -= far[2][e]
 
     def visit(i, carry):
         last = predict(i * together)
@@ -516,7 +542,14 @@
 
     def finish(s, carry):
         for comp in range(8):
-            terms = [grads[s, comp, pl.ds(ROWS * g, ROWS), :] for g in range(groups)]
+            terms = []
+            for g in range(groups):
+                rows = pl.ds(ROWS * g, ROWS)
+                first = grads[s, comp // 2, rows, :]
+                if comp % 2:
+                    terms.append(first + grads[s, 8 + comp // 2, rows, :])
+                else:
+                    terms.append(first - grads[s, 4 + comp // 2, rows, :])
             for n in range(degree_count):
                 if n:
                     terms = [v * x for v, x in zip(terms, xs)]
@@ -546,7 +579,7 @@
         functools.partial(gather_kernel, n),
         out_shape=jax.ShapeDtypeStruct((n, *own.shape), own.dtype),
         in_specs=[pl.BlockSpec(memory_space=pltpu.VMEM)],
-        out_specs=pl.BlockSpec(memory_space=pl.ANY),
+        out_specs=pl.BlockSpec(memory_space=pltpu.HBM),
         scratch_shapes=[
             pltpu.VMEM((n, *own.shape), own.dtype),
             pltpu.SemaphoreType.DMA((n,)),
@@ -563,7 +596,7 @@
     return pl.pallas_call(
         functools.partial(scatter_sum_kernel, n),
         out_shape=jax.ShapeDtypeStruct(piece, parts.dtype),
-        in_specs=[pl.BlockSpec(memory_space=pl.ANY)],
+        in_specs=[pl.BlockSpec(memory_space=pltpu.HBM)],
         out_specs=pl.BlockSpec(memory_space=pltpu.VMEM),
         scratch_shapes=[
             pltpu.VMEM((2, n // 4, *piece), parts.dtype),
@@ -586,9 +619,12 @@
     pairs = uvw.shape[1]
     table = gather(coefficients, n).reshape(n * held, rows, dirs)
     vmem = pl.BlockSpec(memory_space=pltpu.VMEM)
-    away = pl.BlockSpec(memory_space=pl.ANY)
+    away = pl.BlockSpec(memory_space=pltpu.HBM)
     smem = pl.BlockSpec(memory_space=pltpu.SMEM)
-    per_station = pltpu.VMEM((n * held, 8, channels, dirs), jnp.float32)
+
+    def per_station(forms):
+        return pltpu.VMEM((n * held, forms, channels, dirs), jnp.float32)
+
     per_pair = pltpu.VMEM((8, channels, pairs), jnp.float32)
     partial, residual = pl.pallas_call(
         functools.partial(local_kernel, rows // 8, 4),
@@ -600,8 +636,13 @@
         out_specs=(away, vmem),
         scratch_shapes=[pltpu.SMEM(pair.shape, pair.dtype)]
         + [pltpu.VMEM(table.shape, jnp.float32)] * 2
-        + [per_station] * 4
+        + [per_station(12), per_station(8), per_station(8), per_station(12)]
         + [per_pair] * 2
+        + [
+            pltpu.VMEM((8, channels, dirs), jnp.float32),
+            pltpu.VMEM((pairs, dirs), jnp.float32),
+            pltpu.VMEM((2, pairs, dirs), jnp.float32),
+        ]
         + [pltpu.SemaphoreType.DMA, pltpu.SemaphoreType.DMA((4,))],
         compiler_params=pltpu.CompilerParams(vmem_limit_bytes=VMEM_BUDGET),
         name="predict_and_slope",
@@ -613,7 +654,7 @@
 def shards(uvw, directions, brightness, observed, coefficients, pair):
     channels, dirs = brightness.shape[1:]
     stations = lax.axis_size("stn") * coefficients.shape[0]
-    fits = lax.axis_size("stn") % 4 == 0 and 4 * stations * 8 * channels * dirs * 4 <= VMEM_BUDGET // 2
+    fits = lax.axis_size("stn") % 4 == 0 and 40 * stations * channels * dirs * 4 <= VMEM_BUDGET // 2
     if fits and dirs == LANES and uvw.shape[1] == LANES and channels % ROWS == 0:
         return compact_shards(uvw, directions, brightness, observed, coefficients, pair)
     return general_shards(uvw, directions, brightness, observed, coefficients, pair)

time: 56.7 us -> 58.3 us (1.028)
  Pallas kernels: 52 us -> 53.6 us
    pallas_call x1, Pallas kernels: 26.9 us -> 28.5 us  [compact_shards(): pl.pallas_call(functools.partial(local_kernel, rows // 8, 4), out_shape=(...]
where the time goes in v3:
time: 58.3 us; the launch traced here: 58 us
  Pallas kernels  53.6 us (92%)
  local copies, waits for them, and re-layouts  3.73 us (6%)
  between operations  0.74 us (1%)
    pallas_call x1, Pallas kernels, compact_shards(): pl.pallas_call(functools.partial(local_kernel, rows // 8, 4), out_shape=(...  28.5 us
    pallas_call x1, Pallas kernels, gather(): pl.pallas_call(functools.partial(gather_kernel, n), out_shape=jax.ShapeDt...  13.6 us
    pallas_call x1, Pallas kernels, scatter_sum(): pl.pallas_call(functools.partial(scatter_sum_kernel, n), out_shape=jax.Sh...  11.5 us
    unnamed x15, local copies, waits for them, and re-layouts  3.73 us

profile of v3, /device:TPU:0, one launch (start us, length us, event | category | flops | bytes accessed | tf_op | source)
XLA Modules:
  0.0 58.0 jit_solution(6100671486217256770)
XLA Ops:
  0.6 0.0 copy-start.2
  0.6 0.0 copy-start.3
  0.7 0.0 copy-start.4
  0.7 0.0 copy-start.6
  0.7 13.6 %gather_coefficients.1 = f32[16,2,24,128]{3,2,1,0:T(8,128)} custom-call(f32[2,24,128]{2,1,0:T(8,128)} %own_ref.1), custom_call_target="tpu_custom_call" | custom-call | tf_op jit(solution)/shard_map/gather_coefficients/pallas_call | solution.py:578
  14.3 0.0 copy-start.5
  14.3 0.0 copy-done.2
  14.3 0.0 copy-done.3
  14.3 0.0 copy-done.4
  14.3 0.0 copy-done.6
  14.3 0.6 %copy-done.5 = s32[2,128]{1,0:T(2,128)S(1)} copy-done((s32[2,128]{1,0:T(2,128)S(1)}, s32[2,128]{1,0:T(2,128)}, u32[]{:S(2)}) %copy-start.5) | copy-done | bytes 1048
  15.0 0.0 copy-start
  15.0 1.0 %copy-done = f32[16,2,24,128]{3,2,1,0:T(8,128)S(1)} copy-done((f32[16,2,24,128]{3,2,1,0:T(8,128)S(1)}, f32[16,2,24,128]{3,2,1,0:T(8,128)}, u32[]{:S(2)}) %copy-start) | copy-done | bytes 393240
  16.0 28.5 %predict_and_slope.1 = (f32[32,24,128]{2,1,0:T(8,128)S(1)}, f32[256,128]{1,0:T(8,128)}) custom-call(f32[3,128]{1,0:T(4,128)S(1)} %copy-done.4, s32[2,128]{1,0:T(2,128)S(1)} %copy-done.5, f32[2,128]{1,0:T(2,128)S(1)} %copy-done.6, f32[8,32,128]{2,1,0:T(8,128)S(1)} %copy-done.2, f32[256,128]{1,0:T(8,128)S(1)} %bitcast.6, f32[32,24,128]{2,1,0:T(8,128)S(1)} %bitcast.4), custom_call_target="tpu_custom_call" | custom-call | tf_op jit(solution)/shard_map/predict_and_slope/pallas_call | solution.py:629
  44.4 0.0 copy-start.1
  44.4 0.7 %copy-done.1 = f32[32,24,128]{2,1,0:T(8,128)} copy-done((f32[32,24,128]{2,1,0:T(8,128)}, f32[32,24,128]{2,1,0:T(8,128)S(1)}, u32[]{:S(2)}) %copy-start.1) | copy-done | bytes 393240
  45.2 11.5 %sum_gradient.1 = f32[2,24,128]{2,1,0:T(8,128)} custom-call(f32[16,2,24,128]{3,2,1,0:T(8,128)} %bitcast.5), custom_call_target="tpu_custom_call" | custom-call | tf_op jit(solution)/shard_map/sum_gradient/pallas_call | solution.py:596
  56.7 1.3 %copy.9 = f32[2,24,128]{2,1,0:T(8,128)} copy(f32[2,24,128]{2,1,0:T(8,128)} %sum_gradient.1) | data formatting | bytes 49152
Async XLA Ops:
  0.6 13.7 %copy-start.2 = (f32[8,32,128]{2,1,0:T(8,128)S(1)}, f32[8,32,128]{2,1,0:T(8,128)}, u32[]{:S(2)}) copy-start(f32[8,32,128]{2,1,0:T(8,128)} %bright_ref.1) | copy-start | bytes 393220
  0.6 13.7 %copy-start.3 = (f32[32,8,128]{2,1,0:T(8,128)S(1)}, f32[32,8,128]{2,1,0:T(8,128)}, u32[]{:S(2)}) copy-start(f32[32,8,128]{2,1,0:T(8,128)} %param.9) | copy-start | bytes 393220
  0.7 13.7 %copy-start.4 = (f32[3,128]{1,0:T(4,128)S(1)}, f32[3,128]{1,0:T(4,128)}, u32[]{:S(2)}) copy-start(f32[3,128]{1,0:T(4,128)} %uvw_ref.1) | copy-start | bytes 4612
  0.7 13.7 %copy-start.6 = (f32[2,128]{1,0:T(2,128)S(1)}, f32[2,128]{1,0:T(2,128)}, u32[]{:S(2)}) copy-start(f32[2,128]{1,0:T(2,128)} %dir_ref.1) | copy-start | bytes 3076
  14.3 0.7 %copy-start.5 = (s32[2,128]{1,0:T(2,128)S(1)}, s32[2,128]{1,0:T(2,128)}, u32[]{:S(2)}) copy-start(s32[2,128]{1,0:T(2,128)} %pair_hbm.1) | copy-start | bytes 3076
  15.0 1.0 %copy-start = (f32[16,2,24,128]{3,2,1,0:T(8,128)S(1)}, f32[16,2,24,128]{3,2,1,0:T(8,128)}, u32[]{:S(2)}) copy-start(f32[16,2,24,128]{3,2,1,0:T(8,128)} %gather_coefficients.1) | copy-start | bytes 1179652
  44.4 0.7 %copy-start.1 = (f32[32,24,128]{2,1,0:T(8,128)}, f32[32,24,128]{2,1,0:T(8,128)S(1)}, u32[]{:S(2)}) copy-start(f32[32,24,128]{2,1,0:T(8,128)S(1)} %get-tuple-element.4) | copy-start | bytes 1179652

commit v4 on v2

--- a/solution.py
+++ b/solution.py
@@ -11,7 +11,7 @@
 MESH = pl.DeviceIdType.MESH
 LANES = 128
 ROWS = 8
-VMEM_BUDGET = 44 * 1024 * 1024
+VMEM_BUDGET = 64512 * 1024
 
 
 def powers_of(frequency_number, degree_count):
@@ -546,14 +546,14 @@
         functools.partial(gather_kernel, n),
         out_shape=jax.ShapeDtypeStruct((n, *own.shape), own.dtype),
         in_specs=[pl.BlockSpec(memory_space=pltpu.VMEM)],
-        out_specs=pl.BlockSpec(memory_space=pl.ANY),
+        out_specs=pl.BlockSpec(memory_space=pltpu.HBM),
         scratch_shapes=[
             pltpu.VMEM((n, *own.shape), own.dtype),
             pltpu.SemaphoreType.DMA((n,)),
             pltpu.SemaphoreType.DMA((n,)),
             pltpu.SemaphoreType.DMA((n,)),
         ],
-        compiler_params=pltpu.CompilerParams(collective_id=1, has_side_effects=True),
+        compiler_params=pltpu.CompilerParams(collective_id=1, has_side_effects=True, vmem_limit_bytes=VMEM_BUDGET),
         name="gather_coefficients",
     )(own)
 
@@ -563,7 +563,7 @@
     return pl.pallas_call(
         functools.partial(scatter_sum_kernel, n),
         out_shape=jax.ShapeDtypeStruct(piece, parts.dtype),
-        in_specs=[pl.BlockSpec(memory_space=pl.ANY)],
+        in_specs=[pl.BlockSpec(memory_space=pltpu.HBM)],
         out_specs=pl.BlockSpec(memory_space=pltpu.VMEM),
         scratch_shapes=[
             pltpu.VMEM((2, n // 4, *piece), parts.dtype),
@@ -574,7 +574,7 @@
             pltpu.SemaphoreType.DMA((n,)),
             pltpu.SemaphoreType.DMA((n,)),
         ],
-        compiler_params=pltpu.CompilerParams(collective_id=2, has_side_effects=True),
+        compiler_params=pltpu.CompilerParams(collective_id=2, has_side_effects=True, vmem_limit_bytes=VMEM_BUDGET),
         name="sum_gradient",
     )(parts)
 
@@ -586,7 +586,7 @@
     pairs = uvw.shape[1]
     table = gather(coefficients, n).reshape(n * held, rows, dirs)
     vmem = pl.BlockSpec(memory_space=pltpu.VMEM)
-    away = pl.BlockSpec(memory_space=pl.ANY)
+    away = pl.BlockSpec(memory_space=pltpu.HBM)
     smem = pl.BlockSpec(memory_space=pltpu.SMEM)
     per_station = pltpu.VMEM((n * held, 8, channels, dirs), jnp.float32)
     per_pair = pltpu.VMEM((8, channels, pairs), jnp.float32)
@@ -613,7 +613,7 @@
 def shards(uvw, directions, brightness, observed, coefficients, pair):
     channels, dirs = brightness.shape[1:]
     stations = lax.axis_size("stn") * coefficients.shape[0]
-    fits = lax.axis_size("stn") % 4 == 0 and 4 * stations * 8 * channels * dirs * 4 <= VMEM_BUDGET // 2
+    fits = lax.axis_size("stn") % 4 == 0 and 4 * stations * 8 * channels * dirs * 4 <= 22 * 1024 * 1024
     if fits and dirs == LANES and uvw.shape[1] == LANES and channels % ROWS == 0:
         return compact_shards(uvw, directions, brightness, observed, coefficients, pair)
     return general_shards(uvw, directions, brightness, observed, coefficients, pair)

time: 56.7 us -> 55 us (0.970)
  local copies, waits for them, and re-layouts: 3.73 us -> 1.35 us
  Pallas kernels: 52 us -> 52.7 us
    unnamed x15 -> x1, local copies, waits for them, and re-layouts: 3.73 us -> 1.35 us
    pallas_call x1, Pallas kernels: 26.9 us -> 27.6 us  [compact_shards(): pl.pallas_call(functools.partial(local_kernel, rows // 8, 4), out_shape=(...]
where the time goes in v4:
time: 55 us; the launch traced here: 54.7 us
  Pallas kernels  52.7 us (96%)
  local copies, waits for them, and re-layouts  1.35 us (2%)
  between operations  0.65 us (1%)
    pallas_call x1, Pallas kernels, compact_shards(): pl.pallas_call(functools.partial(local_kernel, rows // 8, 4), out_shape=(...  27.6 us
    pallas_call x1, Pallas kernels, gather(): pl.pallas_call(functools.partial(gather_kernel, n), out_shape=jax.ShapeDt...  13.5 us
    pallas_call x1, Pallas kernels, scatter_sum(): pl.pallas_call(functools.partial(scatter_sum_kernel, n), out_shape=jax.Sh...  11.6 us
    unnamed x1, local copies, waits for them, and re-layouts  1.35 us

profile of v4, /device:TPU:0, one launch (start us, length us, event | category | flops | bytes accessed | tf_op | source)
XLA Modules:
  0.0 54.7 jit_solution(1345801653455769097)
XLA Ops:
  0.6 13.5 %gather_coefficients.1 = f32[16,2,24,128]{3,2,1,0:T(8,128)} custom-call(f32[2,24,128]{2,1,0:T(8,128)} %own_ref.1), custom_call_target="tpu_custom_call" | custom-call | tf_op jit(solution)/shard_map/gather_coefficients/pallas_call | solution.py:545
  14.1 27.6 %predict_and_slope.1 = (f32[32,24,128]{2,1,0:T(8,128)}, f32[256,128]{1,0:T(8,128)}) custom-call(f32[3,128]{1,0:T(4,128)} %uvw_ref.1, s32[2,128]{1,0:T(2,128)} %pair_hbm.1, f32[2,128]{1,0:T(2,128)} %dir_ref.1, f32[8,32,128]{2,1,0:T(8,128)} %bright_ref.1, f32[256,128]{1,0:T(8,128)} %bitcast.6, f32[32,24,128]{2,1,0:T(8,128)} %bitcast.4), custom_call_target="tpu_custom_call" | custom-call | tf_op jit(solution)/shard_map/predict_and_slope/pallas_call | solution.py:593
  41.8 11.6 %sum_gradient.1 = f32[2,24,128]{2,1,0:T(8,128)} custom-call(f32[16,2,24,128]{3,2,1,0:T(8,128)} %bitcast.5), custom_call_target="tpu_custom_call" | custom-call | tf_op jit(solution)/shard_map/sum_gradient/pallas_call | solution.py:563
  53.4 1.3 %copy.9 = f32[2,24,128]{2,1,0:T(8,128)} copy(f32[2,24,128]{2,1,0:T(8,128)} %sum_gradient.1) | data formatting | bytes 49152

commit v5 on v3

--- a/solution.py
+++ b/solution.py
@@ -11,7 +11,7 @@
 MESH = pl.DeviceIdType.MESH
 LANES = 128
 ROWS = 8
-VMEM_BUDGET = 44 * 1024 * 1024
+VMEM_BUDGET = 63 * 1024 * 1024
 
 
 def powers_of(frequency_number, degree_count):
@@ -450,7 +450,8 @@
                     with_badj[s, 2 * e + t, rows, :] = d[t][e]
                 for t, form in enumerate((jr, js, jd)):
                     jones[s, 4 * t + e, rows, :] = form[e]
-                    grads[s, 4 * t + e, rows, :] = jnp.zeros(tile, f32)
+                    if t < 2:
+                        grads[s, 4 * t + e, rows, :] = jnp.zeros(tile, f32)
         return carry
 
     lax.fori_loop(0, stations, prepare, 0)
@@ -516,7 +517,8 @@
             ur, ui = [v[0] for v in u], [v[1] for v in u]
             rp, rm = plus(rr, ri), minus(ri, rr)
             near = (real_times(rr, both(u)), real_times(rp, ui), real_times(rm, ur))
-            for k in range(3):
+            near = (minus(near[0], near[1]), plus(near[0], near[2]))
+            for k in range(2):
                 for e in range(4):
                     grads[p, 4 * k + e, rows, :] += near[k][e]
             far = (
@@ -524,10 +526,10 @@
                 real_times(flipped(rm), ti),
                 real_times(flipped(rp), tr),
             )
-            for e in range(4):
-                grads[q, e, rows, :] += far[0][e]
-                grads[q, 4 + e, rows, :] -= far[1][e]
-                grads[q, 8 + e, rows, :] -= far[2][e]
+            far = (plus(far[0], far[1]), minus(far[0], far[2]))
+            for k in range(2):
+                for e in range(4):
+                    grads[q, 4 * k + e, rows, :] += far[k][e]
 
     def visit(i, carry):
         last = predict(i * together)
@@ -542,14 +544,8 @@
 
     def finish(s, carry):
         for comp in range(8):
-            terms = []
-            for g in range(groups):
-                rows = pl.ds(ROWS * g, ROWS)
-                first = grads[s, comp // 2, rows, :]
-                if comp % 2:
-                    terms.append(first + grads[s, 8 + comp // 2, rows, :])
-                else:
-                    terms.append(first - grads[s, 4 + comp // 2, rows, :])
+            slot = 4 * (comp % 2) + comp // 2
+            terms = [grads[s, slot, pl.ds(ROWS * g, ROWS), :] for g in range(groups)]
             for n in range(degree_count):
                 if n:
                     terms = [v * x for v, x in zip(terms, xs)]
@@ -586,7 +582,7 @@
             pltpu.SemaphoreType.DMA((n,)),
             pltpu.SemaphoreType.DMA((n,)),
         ],
-        compiler_params=pltpu.CompilerParams(collective_id=1, has_side_effects=True),
+        compiler_params=pltpu.CompilerParams(collective_id=1, has_side_effects=True, vmem_limit_bytes=VMEM_BUDGET),
         name="gather_coefficients",
     )(own)
 
@@ -607,7 +603,7 @@
             pltpu.SemaphoreType.DMA((n,)),
             pltpu.SemaphoreType.DMA((n,)),
         ],
-        compiler_params=pltpu.CompilerParams(collective_id=2, has_side_effects=True),
+        compiler_params=pltpu.CompilerParams(collective_id=2, has_side_effects=True, vmem_limit_bytes=VMEM_BUDGET),
         name="sum_gradient",
     )(parts)
 
@@ -636,7 +632,7 @@
         out_specs=(away, vmem),
         scratch_shapes=[pltpu.SMEM(pair.shape, pair.dtype)]
         + [pltpu.VMEM(table.shape, jnp.float32)] * 2
-        + [per_station(12), per_station(8), per_station(8), per_station(12)]
+        + [per_station(12), per_station(8), per_station(8), per_station(8)]
         + [per_pair] * 2
         + [
             pltpu.VMEM((8, channels, dirs), jnp.float32),
@@ -654,7 +650,7 @@
 def shards(uvw, directions, brightness, observed, coefficients, pair):
     channels, dirs = brightness.shape[1:]
     stations = lax.axis_size("stn") * coefficients.shape[0]
-    fits = lax.axis_size("stn") % 4 == 0 and 40 * stations * channels * dirs * 4 <= VMEM_BUDGET // 2
+    fits = lax.axis_size("stn") % 4 == 0 and 36 * stations * channels * dirs * 4 <= 22 * 1024 * 1024
     if fits and dirs == LANES and uvw.shape[1] == LANES and channels % ROWS == 0:
         return compact_shards(uvw, directions, brightness, observed, coefficients, pair)
     return general_shards(uvw, directions, brightness, observed, coefficients, pair)

time: 58.3 us -> 55.1 us (0.945)
  local copies, waits for them, and re-layouts: 3.73 us -> 1.35 us
  Pallas kernels: 53.6 us -> 52.8 us
    unnamed x15 -> x1, local copies, waits for them, and re-layouts: 3.73 us -> 1.35 us
    pallas_call x1, Pallas kernels: 28.5 us -> 27.7 us  [compact_shards(): pl.pallas_call(functools.partial(local_kernel, rows // 8, 4), out_shape=(...]
where the time goes in v5:
time: 55.1 us; the launch traced here: 54.8 us
  Pallas kernels  52.8 us (96%)
  local copies, waits for them, and re-layouts  1.35 us (2%)
  between operations  0.65 us (1%)
    pallas_call x1, Pallas kernels, compact_shards(): pl.pallas_call(functools.partial(local_kernel, rows // 8, 4), out_shape=(...  27.7 us
    pallas_call x1, Pallas kernels, gather(): pl.pallas_call(functools.partial(gather_kernel, n), out_shape=jax.ShapeDt...  13.5 us
    pallas_call x1, Pallas kernels, scatter_sum(): pl.pallas_call(functools.partial(scatter_sum_kernel, n), out_shape=jax.Sh...  11.6 us
    unnamed x1, local copies, waits for them, and re-layouts  1.35 us

profile of v5, /device:TPU:0, one launch (start us, length us, event | category | flops | bytes accessed | tf_op | source)
XLA Modules:
  0.0 54.8 jit_solution(2425632090831580368)
XLA Ops:
  0.6 13.5 %gather_coefficients.1 = f32[16,2,24,128]{3,2,1,0:T(8,128)} custom-call(f32[2,24,128]{2,1,0:T(8,128)} %own_ref.1), custom_call_target="tpu_custom_call" | custom-call | tf_op jit(solution)/shard_map/gather_coefficients/pallas_call | solution.py:574
  14.1 27.7 %predict_and_slope.1 = (f32[32,24,128]{2,1,0:T(8,128)}, f32[256,128]{1,0:T(8,128)}) custom-call(f32[3,128]{1,0:T(4,128)} %uvw_ref.1, s32[2,128]{1,0:T(2,128)} %pair_hbm.1, f32[2,128]{1,0:T(2,128)} %dir_ref.1, f32[8,32,128]{2,1,0:T(8,128)} %bright_ref.1, f32[256,128]{1,0:T(8,128)} %bitcast.6, f32[32,24,128]{2,1,0:T(8,128)} %bitcast.4), custom_call_target="tpu_custom_call" | custom-call | tf_op jit(solution)/shard_map/predict_and_slope/pallas_call | solution.py:625
  41.8 11.6 %sum_gradient.1 = f32[2,24,128]{2,1,0:T(8,128)} custom-call(f32[16,2,24,128]{3,2,1,0:T(8,128)} %bitcast.5), custom_call_target="tpu_custom_call" | custom-call | tf_op jit(solution)/shard_map/sum_gradient/pallas_call | solution.py:592
  53.4 1.3 %copy.9 = f32[2,24,128]{2,1,0:T(8,128)} copy(f32[2,24,128]{2,1,0:T(8,128)} %sum_gradient.1) | data formatting | bytes 49152
